TPU v7x, 128 devices: a whole 4x4x4 slice. The times are simulated.
128 devices in a mesh: ctx: 8 (over z, y_hi), exp: 16 (over x, y_lo, core).
Axes of the slice: x: 4, y: 4 (y_hi: 2, y_lo: 2; y = y_hi * 2 + y_lo), z: 4, core: 2. Of those that a mesh axis runs over, the one named last changes fastest.
Arguments:
- queries: bfloat16 [2048, 96, 576], P('ctx', 'exp'), may hold values from -20 to 20
- latent: bfloat16 [2048, 576], P('ctx'), may hold values from -4 to 4
- block_order: int32 [16], replicated, may hold values from 0 to 15, each once
- w_uv: bfloat16 [96, 512, 128], P('exp'), may hold values from -0.75 to 0.75
- w_out: bfloat16 [12288, 7168], P('exp'), may hold values from -0.0546875 to 0.0546875
- resid: bfloat16 [2048, 7168], P(('ctx', 'exp')), may hold values from -3 to 3
- norm_gain: float32 [7168], replicated, may hold values from 0.5 to 1.5
- expert_ids: int32 [2048, 8], P(('ctx', 'exp')), may hold values from 0 to 31, all different within a row; in each aligned block of 16 rows (0 to 15, 16 to 31, ...) at most 6 rows name the same one
- route_weights: float32 [2048, 8], P(('ctx', 'exp')), may hold values from 0.1 to 0.6
- w_gate_up: bfloat16 [32, 7168, 2048], P('exp', 'ctx'), may hold values from -0.0625 to 0.0625
- w_down: bfloat16 [32, 1024, 7168], P('exp', None, 'ctx'), may hold values from -0.1875 to 0.1875
Outputs:
- layer_out: bfloat16 [2048, 7168], P(('ctx', 'exp'))
Inputs may be any that keep to these rules, and one draw needn't show every extreme that they name: `block_order`: A permutation of the 16 stored blocks. `expert_ids`: A token names 8 distinct experts. Among the tokens of one device (aligned blocks of 16 stored rows), no expert is named by more than 6 of them.
All inputs are finite; a program needn't handle non-finite values.
Results may differ from a plain program's by a relative error of at most 0.029.
Values may be sent and summed in bfloat16 or wider, within the bound.
A program may use at most 128 MiB of HBM per device.

v0:
```python
import jax
import jax.numpy as jnp
from jax import lax
from jax.sharding import PartitionSpec as P


def activate(summed_in):
    hidden_units = summed_in.shape[-1] // 2
    return (jax.nn.silu(summed_in[..., :hidden_units]) * summed_in[..., hidden_units:]).astype(
        jnp.bfloat16
    )


def body(
    queries,
    latent,
    block_order,
    w_uv,
    w_out,
    resid,
    norm_gain,
    expert_ids,
    route_weights,
    w_gate_up,
    w_down,
):
    query_count, heads_dev, feat_width = queries.shape
    lat_width = w_uv.shape[1]
    value_width = w_uv.shape[2]
    block_len = query_count // 2
    stored_blocks = block_order.shape[0]
    score_scale = (value_width + feat_width - lat_width) ** (-0.5)
    ctx_rank = lax.axis_index("ctx")

    def seq_positions(first_row, count):
        row_ids = first_row + jnp.arange(count, dtype=jnp.int32)
        block_ids = row_ids // block_len
        match = block_ids[:, None] == jnp.arange(stored_blocks, dtype=jnp.int32)[None, :]
        block_pos = jnp.sum(jnp.where(match, block_order[None, :], 0), axis=1)
        return block_pos * block_len + row_ids % block_len

    query_pos = seq_positions(ctx_rank * query_count, query_count)
    query_rows = queries.reshape(query_count * heads_dev, feat_width)
    query_pos_rows = jnp.repeat(query_pos, heads_dev)
    flat_count = query_count * heads_dev
    keys_part = lax.all_gather(latent, "ctx", axis=0, tiled=True)
    key_pos = seq_positions(jnp.int32(0), keys_part.shape[0])
    top_score = jnp.full((flat_count,), -1e30, jnp.float32)
    scores = (
        lax.dot_general(
            query_rows, keys_part, (((1,), (1,)), ((), ())), preferred_element_type=jnp.float32
        )
        * score_scale
    )
    scores = jnp.where(key_pos[None, :] <= query_pos_rows[:, None], scores, -jnp.inf)
    new_top = jnp.maximum(top_score, jnp.max(scores, axis=1))
    weights = jnp.exp(scores - new_top[:, None])
    value_sum = jnp.dot(
        weights.astype(jnp.bfloat16), keys_part[:, :lat_width], preferred_element_type=jnp.float32
    )
    weight_sum = jnp.sum(weights, axis=1)
    top_score, weight_sum, value_sum = (new_top, weight_sum, value_sum)
    context = (
        (value_sum / weight_sum[:, None])
        .astype(jnp.bfloat16)
        .reshape(query_count, heads_dev, lat_width)
    )
    head_out = jnp.einsum("shl,hlv->shv", context, w_uv, preferred_element_type=jnp.float32).astype(
        jnp.bfloat16
    )
    head_out = head_out.reshape(query_count, heads_dev * value_width)
    tok_count, top_count = expert_ids.shape
    attention = lax.psum_scatter(
        jnp.dot(head_out, w_out, preferred_element_type=jnp.float32).astype(jnp.bfloat16),
        "exp",
        scatter_dimension=0,
        tiled=True,
    ).astype(jnp.float32)
    layer_state = resid.astype(jnp.float32) + attention
    normed = (
        layer_state
        * lax.rsqrt(jnp.mean(layer_state * layer_state, axis=1, keepdims=True) + 1e-06)
        * norm_gain
    ).astype(jnp.bfloat16)
    expert_count = w_gate_up.shape[0] * lax.axis_size("exp")
    capacity = max(2, 3 * tok_count * top_count // (2 * expert_count))
    flat_ids = expert_ids.reshape(-1)
    one_hot = (flat_ids[:, None] == jnp.arange(expert_count, dtype=jnp.int32)[None, :]).astype(
        jnp.int32
    )
    slot_ids = jnp.sum((jnp.cumsum(one_hot, axis=0) - one_hot) * one_hot, axis=1)
    target = flat_ids * capacity + slot_ids
    picker = target[None, :] == jnp.arange(expert_count * capacity, dtype=jnp.int32)[:, None]
    picker = jnp.any(picker.reshape(expert_count * capacity, tok_count, top_count), axis=2).astype(
        jnp.bfloat16
    )
    buffer = jnp.dot(picker, normed, preferred_element_type=jnp.float32).astype(jnp.bfloat16)
    buffer = buffer.reshape(expert_count, 1, capacity, normed.shape[1])
    arrived = lax.all_to_all(
        lax.all_to_all(buffer, "ctx", split_axis=3, concat_axis=1, tiled=True),
        "exp",
        split_axis=0,
        concat_axis=2,
        tiled=True,
    )
    partial_value = jnp.einsum(
        "bcrd,bdh->bcrh", arrived, w_gate_up, preferred_element_type=jnp.float32
    )
    full_sum = lax.psum(partial_value.astype(jnp.bfloat16), "ctx").astype(jnp.float32)
    activated = activate(full_sum)
    replies = jnp.einsum(
        "bcrh,bhd->bcrd", activated, w_down, preferred_element_type=jnp.float32
    ).astype(jnp.bfloat16)
    returned = lax.all_to_all(
        lax.all_to_all(replies, "ctx", split_axis=1, concat_axis=3, tiled=True),
        "exp",
        split_axis=2,
        concat_axis=0,
        tiled=True,
    )
    returned = returned.reshape(expert_count * capacity, normed.shape[1])
    picked = returned[target].reshape(tok_count, top_count, normed.shape[1])
    mixed = jnp.sum(picked.astype(jnp.float32) * route_weights[:, :, None], axis=1)
    return (layer_state + mixed).astype(jnp.bfloat16)


def solution(mesh):
    return jax.shard_map(
        body,
        mesh=mesh,
        in_specs=(
            P("ctx", "exp", None),
            P("ctx", None),
            P(),
            P("exp", None, None),
            P("exp", None),
            P(("ctx", "exp"), None),
            P(),
            P(("ctx", "exp"), None),
            P(("ctx", "exp"), None),
            P("exp", "ctx", None),
            P("exp", None, "ctx"),
        ),
        out_specs=P(("ctx", "exp"), None),
        check_vma=False,
    )
```

profile of v0, /device:TPU:1, one launch (start us, length us, event | category | flops | bytes accessed | tf_op | source)
XLA Modules:
  0.0 683.4 jit_solution(5675584759462062843)
XLA Ops:
  8.3 3.8 copy.60
  14.7 54.6 %all-gather.2.cloned.1.call-done = bf16[2048,576]{0,1:T(8,128)(2,1)} async-done(((bf16[256,576]{0,1:T(8,128)(2,1)}), bf16[2048,576]{0,1:T(8,128)(2,1)}) %all-gather.2.cloned.1.call-update) | async-done | bytes 2359312 | tf_op jit(solution)/shard_map/all_gather | solution.py:46
  69.3 8.4 %fusion.46 = (f32[1536]{0:T(1024)S(1)}, f32[1536,2048]{1,0:T(8,128)S(1)}) fusion(bf16[1536,576]{1,0:T(8,128)(2,1)} %reshape.127, bf16[2048,576]{0,1:T(8,128)(2,1)} %all-gather.2.cloned.1.call-done, s32[1536]{0:T(1024)S(1)} %le.16, s32[2048]{0:T(1024)S(1)} %fusion.39), kind=kOutput, calls=%fused_computation.70 | convolution fusion | flops 3636460032 | bytes 16732160 | tf_op jit(solution)/shard_map/dot_general | solution.py:50
  79.5 5.1 divide_convert_fusion
  87.8 8.9 %convolution_convert_fusion = bf16[256,7168]{1,0:T(8,128)(2,1)} fusion(bf16[256,768]{0,1:T(8,128)(2,1)S(1)} %bitcast.61, bf16[768,7168]{1,0:T(8,128)(2,1)} %param.15), kind=kOutput, calls=%fused_computation.5 | convolution fusion | flops 2820407296 | bytes 15073280 | tf_op jit(solution)/shard_map/dot_general | solution.py:74
  98.3 59.9 %reduce-scatter.2.cloned.1.call-done = bf16[16,7168]{1,0:T(8,128)(2,1)} async-done(((bf16[256,7168]{1,0:T(8,128)(2,1)}), bf16[16,7168]{1,0:T(8,128)(2,1)}) %reduce-scatter.2.cloned.1.call-update) | async-done | bytes 229392 | tf_op jit(solution)/shard_map/reduce_scatter | solution.py:73
  161.2 2.7 reshape.130
  163.9 15.6 %copy.65 = bf16[32,1,6,7168]{0,2,1,3:T(8,128)(2,1)} copy(bf16[32,1,6,7168]{3,2,0,1:T(8,128)(2,1)} %reshape.130) | data formatting | bytes 5505024 | tf_op jit(solution)/shard_map/reshape | solution.py:98
  179.5 12.8 %reshape.144 = bf16[8,2,86016]{2,1,0:T(2,128)(2,1)S(1)} reshape(bf16[7168,1,6,32]{3,2,1,0:T(8,128)(2,1)} %bitcast.55) | data formatting | bytes 5505024
  192.4 37.3 %all_to_all.69 = bf16[8,2,86016]{2,1,0:T(2,128)(2,1)} all-to-all(bf16[8,2,86016]{2,1,0:T(2,128)(2,1)S(1)} %reshape.144), channel_id=1, replica_groups=mesh['ctx'=8,'exp'=16] {'ctx'}, dimensions={0} | all-to-all | bytes 5505024 | tf_op jit(solution)/shard_map/all_to_all | solution.py:100
  229.6 12.1 %reshape.145 = bf16[7168,1,6,32]{3,2,1,0:T(8,128)(2,1)} reshape(bf16[8,2,86016]{2,1,0:T(2,128)(2,1)} %all_to_all.69) | data formatting | bytes 5505024
  241.7 11.5 %copy.67 = bf16[32,8,6,896]{3,1,2,0:T(8,128)(2,1)S(1)} copy(bf16[32,8,6,896]{0,2,3,1:T(8,128)(2,1)} %bitcast.56) | data formatting | bytes 5505024 | tf_op jit(solution)/shard_map/all_to_all | solution.py:100
  253.2 43.9 %all_to_all.70 = bf16[32,8,6,896]{3,1,2,0:T(8,128)(2,1)S(1)} all-to-all(bf16[32,8,6,896]{3,1,2,0:T(8,128)(2,1)S(1)} %copy.67), channel_id=1, replica_groups=mesh['ctx'=8,'exp'=16] {'exp'}, dimensions={0} | all-to-all | bytes 5505024 | tf_op jit(solution)/shard_map/all_to_all | solution.py:99
  297.4 11.6 %fusion.8 = bf16[2,8,96,2048]{3,2,1,0:T(8,128)(2,1)} fusion(bf16[2,896,2048]{2,1,0:T(8,128)(2,1)} %param.20, bf16[2,8,96,896]{3,1,2,0:T(8,128)(2,1)S(1)} %bitcast.60), kind=kOutput, calls=%fused_computation.13 | convolution fusion | flops 5640290304 | bytes 16384000 | tf_op jit(solution)/shard_map/bcrd,bdh->bcrh/dot_general | solution.py:106
  309.0 259.2 %all-reduce.2.cloned.1.call-done = bf16[2,8,96,2048]{3,2,1,0:T(8,128)(2,1)} async-done(((bf16[2,8,96,2048]{3,2,1,0:T(8,128)(2,1)}), bf16[2,8,96,2048]{3,2,1,0:T(8,128)(2,1)}) %all-reduce.2.cloned.1.call-update) | async-done | bytes 6291472 | tf_op jit(solution)/shard_map/psum | solution.py:109
  568.2 4.2 convert_element_type.63
  572.4 5.9 fusion.18
  578.5 38.9 %all_to_all.71 = bf16[2,8,96,896]{3,2,0,1:T(8,128)(2,1)S(1)} all-to-all(bf16[2,8,96,896]{3,2,0,1:T(8,128)(2,1)S(1)} %copy.70), channel_id=1, replica_groups=mesh['ctx'=8,'exp'=16] {'ctx'}, dimensions={1} | all-to-all | bytes 5505024 | tf_op jit(solution)/shard_map/all_to_all | solution.py:115
  621.2 7.5 %all-to-all-start.3 = ((bf16[2,1,96,7168]{3,0,1,2:T(2,128)(2,1)}), bf16[2,1,96,7168]{3,0,1,2:T(2,128)(2,1)S(1)}, u32[]{:S(2)}, u32[]{:S(2)}) async-start(bf16[2,1,96,7168]{3,0,1,2:T(2,128)(2,1)} %reshape.143), calls=%async_computation.4 | async-start | bytes 5505024 | tf_op jit(solution)/shard_map/all_to_all | solution.py:114
  629.0 34.5 %all-to-all-done.3 = bf16[2,1,96,7168]{3,0,1,2:T(2,128)(2,1)S(1)} async-done(((bf16[2,1,96,7168]{3,0,1,2:T(2,128)(2,1)}), bf16[2,1,96,7168]{3,0,1,2:T(2,128)(2,1)S(1)}, u32[]{:S(2)}, u32[]{:S(2)}) %all-to-all-start.3) | async-done | bytes 2752544 | tf_op jit(solution)/shard_map/all_to_all | solution.py:114
  663.5 2.5 copy.73
  666.0 3.2 reshape.131
  669.3 3.0 gather_fusion
  672.2 2.8 fusion.11
  (55 shorter events, 20.2 us)
Async XLA Ops:
  6.5 80.6 %copy-start = (bf16[6,512,128]{2,1,0:T(8,128)(2,1)S(1)}, bf16[6,512,128]{2,1,0:T(8,128)(2,1)}, u32[]{:S(2)}) copy-start(bf16[6,512,128]{2,1,0:T(8,128)(2,1)} %param.14) | copy-start | bytes 2359300
  6.5 62.8 %all-gather.2.cloned.1.call-start = ((), (), s32[]{:S(2)}) async-start(), calls=%async_computation.5 | async-start | bytes 2654208 | tf_op jit(solution)/shard_map/all_gather | solution.py:46
  7.3 150.9 %reduce-scatter.2.cloned.1.call-start = ((), (), s32[]{:S(2)}) async-start(), calls=%async_computation.6 | async-start | bytes 3899392 | tf_op jit(solution)/shard_map/reduce_scatter | solution.py:73
  8.3 6.3 copy-start.6
  77.7 1.8 copy-start.7
  96.7 0.7 copy-start.4
  96.7 61.5 %copy-start.2 = (bf16[16,7168]{1,0:T(8,128)(2,1)S(1)}, bf16[16,7168]{1,0:T(8,128)(2,1)}, u32[]{:S(2)}) copy-start(bf16[16,7168]{1,0:T(8,128)(2,1)} %param.16) | copy-start | bytes 688132
  96.7 62.6 %copy-start.3 = (f32[7168]{0:T(1024)S(1)}, f32[7168]{0:T(1024)}, u32[]{:S(2)}) copy-start(f32[7168]{0:T(1024)} %param.17) | copy-start | bytes 86020
  96.8 471.4 %all-reduce.2.cloned.1.call-start = ((), (), s32[]{:S(2)}) async-start(), calls=%async_computation.7 | async-start | bytes 12582912 | tf_op jit(solution)/shard_map/psum | solution.py:109
  621.2 7.6 %copy-start.5 = (f32[16,8]{0,1:T(8,128)S(1)}, f32[16,8]{0,1:T(8,128)}, u32[]{:S(2)}) copy-start(f32[16,8]{0,1:T(8,128)} %param.19) | copy-start | bytes 1540
  621.2 42.2 %all-to-all-start.3 = ((bf16[2,1,96,7168]{3,0,1,2:T(2,128)(2,1)}), bf16[2,1,96,7168]{3,0,1,2:T(2,128)(2,1)S(1)}, u32[]{:S(2)}, u32[]{:S(2)}) async-start(bf16[2,1,96,7168]{3,0,1,2:T(2,128)(2,1)} %reshape.143), calls=%async_computation.4 | async-start | bytes 5505024 | tf_op jit(solution)/shard_map/all_to_all | solution.py:114
  669.3 7.6 %copy-start.1 = (bf16[6,512,128]{2,1,0:T(8,128)(2,1)S(1)}, bf16[6,512,128]{2,1,0:T(8,128)(2,1)}, u32[]{:S(2)}) copy-start(bf16[6,512,128]{2,1,0:T(8,128)(2,1)} %param.14) | copy-start | bytes 2359300
Sparse Core Ops, SparseCore 0:
  9.5 59.7 all-gather.1
  96.9 61.2 reduce-scatter.1
  309.1 259.0 all-reduce.1
where the time goes:
time: 687 us; the launch traced here: 683 us
  waiting for transfers between devices  409 us (60%)
  blocking collectives  120 us (17%)
  local copies, waits for them, and re-layouts  77.8 us (11%)
  matrix products  42.4 us (6%)
  between operations  13.3 us (2%)
  other arithmetic  13.2 us (2%)
  starting transfers between devices  7.62 us (1%)
    psum x1, waiting for transfers between devices, body(): lax.psum(partial_value.astype(jnp.bfloat16), 'ctx').astype(jnp.float32)  259 us
    reduce_scatter x1, waiting for transfers between devices, body(): lax.psum_scatter(jnp.dot(head_out, w_out, preferred_element_type=jnp.floa...  59.9 us
    all_gather x1, waiting for transfers between devices, body(): keys_part = lax.all_gather(latent, 'ctx', axis=0, tiled=True)  54.6 us
    all_to_all x1, blocking collectives, body(): lax.all_to_all(lax.all_to_all(buffer, 'ctx', split_axis=3, concat_axis=1,...  43.9 us
    all_to_all x1, blocking collectives, body(): lax.all_to_all(replies, 'ctx', split_axis=1, concat_axis=3, tiled=True)  38.9 us
    all_to_all x1, blocking collectives, body(): lax.all_to_all(buffer, 'ctx', split_axis=3, concat_axis=1, tiled=True)  37.3 us
    all_to_all x1, waiting for transfers between devices, body(): lax.all_to_all(lax.all_to_all(replies, 'ctx', split_axis=1, concat_axis=3...  34.5 us
    unnamed x21, local copies, waits for them, and re-layouts  29.5 us
  transfers between devices with their start and end apart: 4, of which 4 were waited for; matrix products, arithmetic and copies ran while one was open for 1% of the time, Pallas kernels for 0%

commit v1 on v0

v1 whole, which is shorter than its diff:
```python
import functools

import jax
import jax.numpy as jnp
from jax import lax
from jax.experimental import pallas as pl
from jax.experimental.pallas import tpu as pltpu
from jax.sharding import PartitionSpec as P

BF = jnp.bfloat16
F32 = jnp.float32
DMA = pltpu.SemaphoreType.DMA
W = 896


def place():
    c = lax.axis_index("ctx")
    e = lax.axis_index("exp")
    return c // 2, c % 2, e // 4, (e // 2) % 2, e % 2


def dev(z, yh, x, yl, co):
    return (z * 2 + yh, x * 4 + yl * 2 + co)


def put(src, dst, ss, rs, device):
    return pltpu.make_async_remote_copy(
        src_ref=src,
        dst_ref=dst,
        send_sem=ss,
        recv_sem=rs,
        device_id=device,
        device_id_type=pl.DeviceIdType.MESH,
    )


def greet(devices):
    barrier = pltpu.get_barrier_semaphore()
    for d in devices:
        pl.semaphore_signal(barrier, inc=1, device_id=d, device_id_type=pl.DeviceIdType.MESH)
    pl.semaphore_wait(barrier, len(devices))


def exp_peers(pos):
    z, yh, x, yl, co = pos
    core = dev(z, yh, x, yl, (co + 1) % 2)
    ylp = dev(z, yh, x, (yl + 1) % 2, co)
    xs = [dev(z, yh, (x + d) % 4, yl, co) for d in (1, 2, 3)]
    return core, ylp, xs


REDUCE_SCRATCH = [
    pltpu.VMEM((8, 4, 2, 16, W), F32),
    pltpu.VMEM((8, 4, 2, 16, W), BF),
    pltpu.VMEM((8, 4, 2, 16, W), BF),
    pltpu.VMEM((8, 4, 2, 16, W), BF),
    pltpu.VMEM((4, 3, 2, 16, W), BF),
    pltpu.VMEM((4, 4, 16, W), BF),
    pltpu.VMEM((4, 16, W), BF),
    pltpu.VMEM((4, 3, 16, W), BF),
    pltpu.VMEM((4, 16, W), BF),
    pltpu.VMEM((4, 3, 16, W), BF),
    pltpu.VMEM((8, 16, W), F32),
    DMA((8,)),
    DMA((8,)),
    DMA((4, 3)),
    DMA((4, 3)),
    DMA((4,)),
    DMA((4,)),
    DMA((4,)),
    DMA((4,)),
    DMA((4, 3)),
    DMA((4, 3)),
]


class Reduce:
    def __init__(self, refs, pos):
        (self.own, self.cs, self.cl, self.s1, self.x1, self.y1, self.y2s, self.x2s, self.y2,
         self.x2, self.acc, *self.sems) = refs
        self.pos = pos
        self.core, self.ylp, self.xs = exp_peers(pos)

    def c_core(self, n):
        return put(self.cs.at[n], self.cl.at[n], self.sems[0].at[n], self.sems[1].at[n], self.core)

    def c_x1(self, i, d):
        xx = (self.pos[2] + d) % 4
        return put(self.s1.at[2 * i, xx], self.x1.at[i, d - 1], self.sems[2].at[i, d - 1],
                   self.sems[3].at[i, d - 1], self.xs[d - 1])

    def c_y1(self, i):
        return put(self.s1.at[2 * i + 1, :, (self.pos[3] + 1) % 2], self.y1.at[i], self.sems[4].at[i],
                   self.sems[5].at[i], self.ylp)

    def c_y2(self, i):
        return put(self.y2s.at[i], self.y2.at[i], self.sems[6].at[i], self.sems[7].at[i], self.ylp)

    def c_x2(self, i, d):
        return put(self.x2s.at[i, d - 1], self.x2.at[i, d - 1], self.sems[8].at[i, d - 1],
                   self.sems[9].at[i, d - 1], self.xs[d - 1])

    def chip_sum(self, n):
        self.c_core(n).wait_recv()
        self.s1[n] = (self.own[n] + self.cl[n].astype(F32)).astype(BF)

    def first(self, i):
        self.chip_sum(2 * i)
        for d in (1, 2, 3):
            self.c_x1(i, d).start()
        self.chip_sum(2 * i + 1)
        self.c_y1(i).start()

    def second(self, i):
        x, yl = self.pos[2], self.pos[3]
        yo = (yl + 1) % 2
        for d in (1, 2, 3):
            self.c_x1(i, d).wait_recv()

        def over_x(which):
            t = self.s1[2 * i, x, which].astype(F32)
            for d in (0, 1, 2):
                t = t + self.x1[i, d, which].astype(F32)
            return t

        self.y2s[i] = over_x(yo).astype(BF)
        self.c_y2(i).start()
        self.acc[2 * i] = over_x(yl)
        self.c_y1(i).wait_recv()
        for d in (1, 2, 3):
            xx = (x + d) % 4
            t = self.s1[2 * i + 1, xx, yl].astype(F32) + self.y1[i, xx].astype(F32)
            self.x2s[i, d - 1] = t.astype(BF)
            self.c_x2(i, d).start()
        self.acc[2 * i + 1] = self.s1[2 * i + 1, x, yl].astype(F32) + self.y1[i, x].astype(F32)

    def third(self, i):
        self.c_y2(i).wait_recv()
        self.acc[2 * i] = self.acc[2 * i] + self.y2[i].astype(F32)
        t = self.acc[2 * i + 1]
        for d in (1, 2, 3):
            self.c_x2(i, d).wait_recv()
            t = t + self.x2[i, d - 1].astype(F32)
        self.acc[2 * i + 1] = t

    def drain(self, i):
        self.c_core(2 * i).wait_send()
        self.c_core(2 * i + 1).wait_send()
        self.c_y1(i).wait_send()
        self.c_y2(i).wait_send()
        for d in (1, 2, 3):
            self.c_x1(i, d).wait_send()
            self.c_x2(i, d).wait_send()


def loop(count, step):
    def body(k, carry):
        step(k)
        return carry

    lax.fori_loop(0, count, body, 0)


def when(cond):
    return pl.when(cond)


def project_kernel(heads, w_hbm, resid, gain, state, normed, w, wsem, *reduce_refs):
    pos = place()
    core, ylp, xs = exp_peers(pos)

    def load(n):
        return pltpu.make_async_copy(
            w_hbm.at[:, pl.ds(pl.multiple_of(n * W, W), W)], w.at[n], wsem.at[n]
        )

    loop(8, lambda n: load(n).start())
    greet([core, ylp] + xs)
    red = Reduce(reduce_refs, pos)

    def multiply(n):
        load(n).wait()
        t = jnp.dot(heads[...], w[n], preferred_element_type=F32)
        red.cs[n] = t[:128].astype(BF).reshape(4, 2, 16, W)
        red.c_core(n).start()
        red.own[n] = t[128:].reshape(4, 2, 16, W)

    def step(k):
        @when(k < 4)
        def _():
            multiply(2 * k)
            multiply(2 * k + 1)

        @when((k >= 1) & (k < 5))
        def _():
            red.first(k - 1)

        @when((k >= 2) & (k < 6))
        def _():
            red.second(k - 2)

        @when(k >= 3)
        def _():
            red.third(k - 3)

    loop(7, step)
    square = jnp.zeros((16, 1), F32)
    for n in range(8):
        t = resid[:, n * W:(n + 1) * W].astype(F32) + red.acc[n]
        state[n] = t
        square = square + jnp.sum(t * t, axis=1, keepdims=True)
    scale = lax.rsqrt(square / (8 * W) + 1e-06)
    for n in range(8):
        normed[n] = (state[n] * scale * gain[:, n * W:(n + 1) * W]).astype(BF)
    loop(4, red.drain)


def experts_kernel(normed, slots, weights, state, wg_hbm, wd_hbm, out,
                   wg, wd, wsem, xb, rows, abuf, la, bbuf, bown, lb1, b2, lb2, a2, la2, suma,
                   acta, actb, yrow, tbuf, fin, ret, sems, *reduce_refs):
    pos = place()
    z, yh, x, yl, co = pos
    me = z * 2 + yh
    core, ylp, xs = exp_peers(pos)
    yo = (yl + 1) % 2
    yp = dev(z, (yh + 1) % 2, x, yl, co)
    zs = [dev((z + d) % 4, yh, x, yl, co) for d in (1, 2, 3)]
    red = Reduce(reduce_refs, pos)
    (s_in, r_in, s_g1x, r_g1x, s_g1y, r_g1y, s_g2y, r_g2y, s_g2x, r_g2x, s_gc, r_gc,
     s_a1, r_a1, s_b1, r_b1, s_b2, r_b2, s_a2, r_a2, s_ay, r_ay, s_az, r_az, s_bz, r_bz, s_by, r_by,
     s_f, r_f) = sems

    loads = [
        pltpu.make_async_copy(wg_hbm.at[0], wg.at[0], wsem.at[0]),
        pltpu.make_async_copy(wg_hbm.at[1], wg.at[1], wsem.at[1]),
        pltpu.make_async_copy(wd_hbm, wd, wsem.at[2]),
    ]
    for cp in loads:
        cp.start()
    ctx = [dev((z + dz) % 4, (yh + dy) % 2, x, yl, co) for dz in range(4) for dy in range(2) if dz or dy]
    greet([core, ylp] + xs + ctx)

    def chunk(dz, dy):
        return ((z + 4 - dz) % 4) * 2 + (yh + dy) % 2

    def c_in(dz, dy):
        zz, yy = (z + dz) % 4, (yh + dy) % 2
        r = dz * 2 + dy
        return put(normed.at[zz * 2 + yy], xb.at[me, co, x, yl], s_in.at[r], r_in.at[r],
                   dev(zz, yy, x, yl, co))

    for dz in (1, 2, 3, 0):
        for dy in range(2):
            if dz or dy:
                c_in(dz, dy).start()
    xb[me, co, x, yl] = normed[me]

    def c_g1x(dz, d):
        c = chunk(dz, 0)
        return put(xb.at[c, co, x, yl], xb.at[c, co, x, yl], s_g1x.at[dz, d - 1], r_g1x.at[dz, d - 1], xs[d - 1])

    def c_g2y(dz):
        c = chunk(dz, 0)
        return put(xb.at[c, co, :, yl], xb.at[c, co, :, yl], s_g2y.at[dz], r_g2y.at[dz], ylp)

    def c_g1y(dz):
        c = chunk(dz, 1)
        return put(xb.at[c, co, x, yl], xb.at[c, co, x, yl], s_g1y.at[dz], r_g1y.at[dz], ylp)

    def c_g2x(dz, d):
        c = chunk(dz, 1)
        return put(xb.at[c, co, x], xb.at[c, co, x], s_g2x.at[dz, d - 1], r_g2x.at[dz, d - 1], xs[d - 1])

    def c_gc(dz, dy):
        c = chunk(dz, dy)
        return put(xb.at[c, co], xb.at[c, co], s_gc.at[dz, dy], r_gc.at[dz, dy], core)

    def gather1(dz):
        @when(dz > 0)
        def _():
            c_in(dz, 0).wait_recv()
        for d in (1, 2, 3):
            c_g1x(dz, d).start()
        c_in(dz, 1).wait_recv()
        c_g1y(dz).start()

    def gather2(dz):
        for d in (1, 2, 3):
            c_g1x(dz, d).wait_recv()
        c_g2y(dz).start()
        c_g1y(dz).wait_recv()
        for d in (1, 2, 3):
            c_g2x(dz, d).start()

    def gather3(dz):
        c_g2y(dz).wait_recv()
        c_gc(dz, 0).start()
        for d in (1, 2, 3):
            c_g2x(dz, d).wait_recv()
        c_gc(dz, 1).start()

    def c_a1(dz, d):
        return put(abuf.at[dz], la.at[d - 1], s_a1.at[d - 1], r_a1.at[d - 1],
                   dev((z + 4 - d) % 4, yh, x, yl, co))

    def c_b1(dz):
        return put(bbuf.at[dz], lb1.at[dz], s_b1.at[dz], r_b1.at[dz], yp)

    def c_b2(dz):
        return put(b2.at[dz], lb2.at[dz], s_b2.at[dz], r_b2.at[dz], dev((z + 4 - dz) % 4, yh, x, yl, co))

    row_id = lax.broadcasted_iota(jnp.int32, (96, 256), 0)

    def gate_up(dz):
        for dy in range(2):
            c_gc(dz, dy).wait_recv()
            c = chunk(dz, dy)
            tokens = xb[c].reshape(256, W)
            for i in range(2):
                pick = (row_id == slots[c, i:i + 1, :]).astype(BF)
                rows[i, dy * 96:(dy + 1) * 96] = jnp.dot(pick, tokens, preferred_element_type=F32).astype(BF)

        def cols(t):
            sl = pl.ds(pl.multiple_of(t * 512, 512), 512)
            r = jnp.dot(rows[0], wg[0, :, sl], preferred_element_type=F32).astype(BF)
            abuf[dz, :, :, sl] = r.reshape(2, 96, 512)

        loop(4, cols)

        for d in (1, 2, 3):
            @when(dz == d)
            def _():
                c_a1(d, d).start()

        def cols(t):
            sl = pl.ds(pl.multiple_of(t * 512, 512), 512)
            r = jnp.dot(rows[1], wg[1, :, sl], preferred_element_type=F32).astype(BF)
            bown[dz, :, sl] = r[:96]
            bbuf[dz, :, sl] = r[96:]

        loop(4, cols)
        c_b1(dz).start()

    def forward_b(dz):
        c_b1(dz).wait_recv()

        def cols(t):
            sl = pl.ds(pl.multiple_of(t * 512, 512), 512)
            b2[dz, :, sl] = (bown[dz, :, sl].astype(F32) + lb1[dz, :, sl].astype(F32)).astype(BF)

        loop(4, cols)

        @when(dz > 0)
        def _():
            c_b2(dz).start()

    def order(k):
        return (k + 1) % 4

    def step(k):
        @when(k < 4)
        def _():
            gather1(order(k))

        @when((k >= 1) & (k < 5))
        def _():
            gather2(order(k - 1))

        @when((k >= 2) & (k < 6))
        def _():
            gather3(order(k - 2))

        @when(k == 3)
        def _():
            loads[0].wait()
            loads[1].wait()

        @when((k >= 3) & (k < 7))
        def _():
            gate_up(order(k - 3))

        @when(k >= 5)
        def _():
            forward_b(order(k - 5))

    loop(9, step)

    for d in (1, 2, 3):
        c_a1(d, d).wait_recv()

    def cols(t):
        sl = pl.ds(pl.multiple_of(t * 256, 256), 256)

        def total(dy):
            r = abuf[0, dy, :, sl].astype(F32)
            for d in range(3):
                r = r + la[d, dy, :, sl].astype(F32)
            return r

        a2[:, sl] = total(1).astype(BF)
        suma[:, sl] = total(0)

    loop(8, cols)
    c_a2 = put(a2, la2, s_a2, r_a2, yp)
    c_a2.start()

    def activate(gate, up):
        return (gate / (1.0 + jnp.exp(-gate)) * up).astype(BF)

    c_a2.wait_recv()

    def cols(t):
        lo = pl.ds(pl.multiple_of(t * 256, 256), 256)
        hi = pl.ds(pl.multiple_of(t * 256 + 1024, 256), 256)
        acta[z, yh, :, lo] = activate(suma[:, lo] + la2[:, lo].astype(F32), suma[:, hi] + la2[:, hi].astype(F32))

    loop(4, cols)
    c_ay = put(acta.at[z, yh], acta.at[z, yh], s_ay, r_ay, yp)
    c_ay.start()

    def c_az(d):
        return put(acta.at[z], acta.at[z], s_az.at[d - 1], r_az.at[d - 1], zs[d - 1])

    def c_bz(d):
        return put(actb.at[z, yh], actb.at[z, yh], s_bz.at[d - 1], r_bz.at[d - 1], zs[d - 1])

    def c_by(dz):
        zz = (z + 4 - dz) % 4
        return put(actb.at[zz, yh], actb.at[zz, yh], s_by.at[dz], r_by.at[dz], yp)

    c_ay.wait_recv()
    for d in (1, 2, 3):
        c_az(d).start()

    for d in (1, 2, 3):
        c_b2(d).wait_recv()

    def cols(t):
        lo = pl.ds(pl.multiple_of(t * 256, 256), 256)
        hi = pl.ds(pl.multiple_of(t * 256 + 1024, 256), 256)

        def total(sl):
            r = b2[0, :, sl].astype(F32)
            for d in (1, 2, 3):
                r = r + lb2[d, :, sl].astype(F32)
            return r

        actb[z, yh, :, lo] = activate(total(lo), total(hi))

    loop(4, cols)
    for d in (1, 2, 3):
        c_bz(d).start()
    loads[2].wait()

    def pass_on(dz):
        for d in (1, 2, 3):
            @when(dz == d)
            def _():
                c_bz(d).wait_recv()
        c_by(dz).start()

    def down(dz):
        zz = (z + 4 - dz) % 4
        for d in (1, 2, 3):
            @when(dz == d)
            def _():
                c_az(d).wait_recv()
        c_by(dz).wait_recv()
        yrow[0] = jnp.dot(acta[zz].reshape(192, 1024), wd[0], preferred_element_type=F32).astype(BF)
        yrow[1] = jnp.dot(actb[zz].reshape(192, 1024), wd[1], preferred_element_type=F32).astype(BF)
        for dy in range(2):
            yy = (yh + dy) % 2
            c = zz * 2 + yy
            t = jnp.zeros((256, W), F32)
            for i in range(2):
                pick = jnp.where(row_id == slots[c, i:i + 1, :], weights[c, i:i + 1, :], 0.0).astype(BF)
                t = t + lax.dot_general(
                    pick, yrow[i, pl.ds(pl.multiple_of(yy * 96, 96), 96)], (((0,), (0,)), ((), ())),
                    preferred_element_type=F32)
            tbuf[...] = t.reshape(2, 4, 2, 16, W)
            n = dz * 2 + dy
            red.cs[n] = tbuf[(co + 1) % 2].astype(BF)
            red.c_core(n).start()
            red.own[n] = tbuf[co]

    def c_f(dz, dy):
        c = chunk(dz, dy)
        r = dz * 2 + dy
        return put(fin.at[r], ret.at[me], s_f.at[r], r_f.at[r],
                   dev((z + 4 - dz) % 4, (yh + dy) % 2, x, yl, co))

    def send_back(dz):
        red.third(dz)
        for dy in range(2):
            n = dz * 2 + dy
            fin[n] = red.acc[n].astype(BF)
            if dy:
                c_f(dz, dy).start()
            else:
                @when(dz > 0)
                def _():
                    c_f(dz, dy).start()

    def step(k):
        @when(k < 4)
        def _():
            pass_on(k)

        @when((k >= 1) & (k < 5))
        def _():
            down(k - 1)

        @when((k >= 2) & (k < 6))
        def _():
            red.first(k - 2)

        @when((k >= 3) & (k < 7))
        def _():
            red.second(k - 3)

        @when(k >= 4)
        def _():
            send_back(k - 4)

    loop(8, step)
    ret[me] = fin[0]
    for r in range(1, 8):
        c_f(r // 2, r % 2).wait_recv()
    for n in range(8):
        out[:, n * W:(n + 1) * W] = (state[n] + ret[n].astype(F32)).astype(BF)

    loop(4, red.drain)
    for r in range(1, 8):
        c_f(r // 2, r % 2).wait_send()
        c_in(r // 2, r % 2).wait_send()
    for dz in range(4):
        for d in (1, 2, 3):
            c_g1x(dz, d).wait_send()
            c_g2x(dz, d).wait_send()
        c_g1y(dz).wait_send()
        c_g2y(dz).wait_send()
        c_gc(dz, 0).wait_send()
        c_gc(dz, 1).wait_send()
        c_b1(dz).wait_send()
        c_by(dz).wait_send()
    for d in (1, 2, 3):
        c_a1(d, d).wait_send()
        c_b2(d).wait_send()
        c_az(d).wait_send()
        c_bz(d).wait_send()
    c_a2.wait_send()
    c_ay.wait_send()


VM = pl.BlockSpec(memory_space=pltpu.VMEM)
ANY = pl.BlockSpec(memory_space=pl.ANY)


def project(heads, w_out, resid, gain):
    return pl.pallas_call(
        project_kernel,
        name="project",
        out_shape=(jax.ShapeDtypeStruct((8, 16, W), F32), jax.ShapeDtypeStruct((8, 16, W), BF)),
        in_specs=[VM, ANY, VM, VM],
        out_specs=(VM, VM),
        scratch_shapes=[pltpu.VMEM((8, 768, W), BF), DMA((8,))] + REDUCE_SCRATCH,
        compiler_params=pltpu.CompilerParams(
            collective_id=1, has_side_effects=True, vmem_limit_bytes=50 << 20),
    )(heads, w_out, resid, gain)


def experts(normed, slots, weights, state, w_gate_up, w_down):
    hid2 = w_gate_up.shape[2]
    hid = hid2 // 2
    sems = [
        DMA((8,)), DMA((8,)),
        DMA((4, 3)), DMA((4, 3)), DMA((4,)), DMA((4,)), DMA((4,)), DMA((4,)), DMA((4, 3)), DMA((4, 3)),
        DMA((4, 2)), DMA((4, 2)),
        DMA((3,)), DMA((3,)), DMA((4,)), DMA((4,)), DMA((4,)), DMA((4,)), DMA, DMA,
        DMA, DMA, DMA((3,)), DMA((3,)), DMA((3,)), DMA((3,)), DMA((4,)), DMA((4,)),
        DMA((8,)), DMA((8,)),
    ]
    return pl.pallas_call(
        experts_kernel,
        name="experts",
        out_shape=jax.ShapeDtypeStruct((16, 8 * W), BF),
        in_specs=[VM, VM, VM, VM, ANY, ANY],
        out_specs=VM,
        scratch_shapes=[
            pltpu.VMEM((2, W, hid2), BF),
            pltpu.VMEM((2, hid, W), BF),
            DMA((3,)),
            pltpu.VMEM((8, 2, 4, 2, 16, W), BF),
            pltpu.VMEM((2, 192, W), BF),
            pltpu.VMEM((4, 2, 96, hid2), BF),
            pltpu.VMEM((3, 2, 96, hid2), BF),
            pltpu.VMEM((4, 96, hid2), BF),
            pltpu.VMEM((4, 96, hid2), BF),
            pltpu.VMEM((4, 96, hid2), BF),
            pltpu.VMEM((4, 96, hid2), BF),
            pltpu.VMEM((4, 96, hid2), BF),
            pltpu.VMEM((96, hid2), BF),
            pltpu.VMEM((96, hid2), BF),
            pltpu.VMEM((96, hid2), F32),
            pltpu.VMEM((4, 2, 96, hid), BF),
            pltpu.VMEM((4, 2, 96, hid), BF),
            pltpu.VMEM((2, 192, W), BF),
            pltpu.VMEM((2, 4, 2, 16, W), F32),
            pltpu.VMEM((8, 16, W), BF),
            pltpu.VMEM((8, 16, W), BF),
            tuple(sems),
        ] + REDUCE_SCRATCH,
        compiler_params=pltpu.CompilerParams(
            collective_id=2, has_side_effects=True, vmem_limit_bytes=62 << 20),
    )(normed, slots, weights, state, w_gate_up, w_down)


def routing(expert_ids, route_weights):
    e = lax.axis_index("exp")
    both = jnp.concatenate([expert_ids.astype(F32), route_weights], axis=1)
    every = lax.all_gather(both, ("ctx", "exp"), axis=0, tiled=True)
    mine = (2 * e + jnp.arange(2)).astype(F32)
    match = every[None, :, :8] == mine[:, None, None]
    hit = jnp.any(match, axis=2)
    weight = jnp.sum(jnp.where(match, every[None, :, 8:], 0.0), axis=2)
    hit = hit.reshape(2, 8, 4, 2, 2, 16)
    before = jnp.arange(16)[:, None] > jnp.arange(16)[None, :]
    rank = jnp.sum(jnp.where(before & hit[..., None, :], 1, 0), axis=-1)
    hit, rank, weight = (
        jnp.transpose(t.reshape(2, 8, 4, 2, 2, 16), (1, 0, 4, 2, 3, 5)).reshape(8, 2, 16, 16)
        for t in (hit, rank, weight)
    )
    slot = jnp.where(hit, jnp.arange(16)[:, None] * 6 + rank, -1)
    return slot.reshape(8, 2, 256).astype(jnp.int32), weight.reshape(8, 2, 256)


def attend(queries, latent, block_order, w_uv):
    query_count, heads_dev, feat_width = queries.shape
    lat_width = w_uv.shape[1]
    value_width = w_uv.shape[2]
    block_len = query_count // 2
    stored_blocks = block_order.shape[0]
    score_scale = (value_width + feat_width - lat_width) ** (-0.5)
    ctx_rank = lax.axis_index("ctx")

    def seq_positions(first_row, count):
        row_ids = first_row + jnp.arange(count, dtype=jnp.int32)
        block_ids = row_ids // block_len
        match = block_ids[:, None] == jnp.arange(stored_blocks, dtype=jnp.int32)[None, :]
        block_pos = jnp.sum(jnp.where(match, block_order[None, :], 0), axis=1)
        return block_pos * block_len + row_ids % block_len

    query_pos = seq_positions(ctx_rank * query_count, query_count)
    query_rows = queries.reshape(query_count * heads_dev, feat_width)
    query_pos_rows = jnp.repeat(query_pos, heads_dev)
    keys = lax.all_gather(latent, "ctx", axis=0, tiled=True)
    key_pos = seq_positions(jnp.int32(0), keys.shape[0])
    scores = (
        lax.dot_general(query_rows, keys, (((1,), (1,)), ((), ())), preferred_element_type=F32) * score_scale
    )
    scores = jnp.where(key_pos[None, :] <= query_pos_rows[:, None], scores, -jnp.inf)
    weights = jnp.exp(scores - jnp.max(scores, axis=1)[:, None])
    value_sum = jnp.dot(weights.astype(BF), keys[:, :lat_width], preferred_element_type=F32)
    weight_sum = jnp.sum(weights, axis=1)
    context = (value_sum / weight_sum[:, None]).astype(BF).reshape(query_count, heads_dev, lat_width)
    head_out = jnp.einsum("shl,hlv->shv", context, w_uv, preferred_element_type=F32).astype(BF)
    return head_out.reshape(query_count, heads_dev * value_width)


def body(queries, latent, block_order, w_uv, w_out, resid, norm_gain, expert_ids, route_weights, w_gate_up, w_down):
    slots, weights = routing(expert_ids, route_weights)
    head_out = attend(queries, latent, block_order, w_uv)
    by_core = head_out.reshape(8, 2, 16, -1).transpose(1, 0, 2, 3)
    by_core = jnp.where(lax.axis_index("exp") % 2 == 0, by_core[::-1], by_core).reshape(256, -1)
    state, normed = project(by_core, w_out, resid, norm_gain.reshape(1, -1))
    return experts(normed, slots, weights, state, w_gate_up, w_down)


def solution(mesh):
    return jax.shard_map(
        body,
        mesh=mesh,
        in_specs=(
            P("ctx", "exp", None),
            P("ctx", None),
            P(),
            P("exp", None, None),
            P("exp", None),
            P(("ctx", "exp"), None),
            P(),
            P(("ctx", "exp"), None),
            P(("ctx", "exp"), None),
            P("exp", "ctx", None),
            P("exp", None, "ctx"),
        ),
        out_specs=P(("ctx", "exp"), None),
        check_vma=False,
    )
```

time: 687 us -> 402 us (0.59)
  waiting for transfers between devices: 409 us -> 0.71 us
  Pallas kernels: 0 us -> 164 us
  blocking collectives: 120 us -> 184 us
  local copies, waits for them, and re-layouts: 77.8 us -> 15.7 us
  matrix products: 42.4 us -> 14.8 us
  starting transfers between devices: 7.62 us -> 0.01 us
    psum x1 -> x0, waiting for transfers between devices: 259 us -> none  [body(): lax.psum(partial_value.astype(jnp.bfloat16), 'ctx').astype(jnp.float32)]
    all_gather x0 -> x1, blocking collectives: none -> 184 us  [routing(): every = lax.all_gather(both, ('ctx', 'exp'), axis=0, tiled=True)]
    pallas_call x0 -> x2, Pallas kernels: none -> 164 us  [the longest x1 141 us: experts(): pl.pallas_call(experts_kernel, name='experts', out_shape=jax.ShapeDtypeSt...]
    all_to_all x3 -> x0, blocking collectives: 120 us -> none  [the longest x1 43.9 us: body(): lax.all_to_all(lax.all_to_all(buffer, 'ctx', split_axis=3, concat_axis=1,...]
    reduce_scatter x1 -> x0, waiting for transfers between devices: 59.9 us -> none  [body(): lax.psum_scatter(jnp.dot(head_out, w_out, preferred_element_type=jnp.floa...]
    all_gather x1, waiting for transfers between devices: 54.6 us -> 0.01 us  [attend(): keys = lax.all_gather(latent, 'ctx', axis=0, tiled=True)]
    all_to_all x1 -> x0, waiting for transfers between devices: 34.5 us -> none  [body(): lax.all_to_all(lax.all_to_all(replies, 'ctx', split_axis=1, concat_axis=3...]
    dot_general x7 -> x3, matrix products: 42.4 us -> 14.8 us  [the longest x1 8.56 us: attend(): lax.dot_general(query_rows, keys, (((1,), (1,)), ((), ())), preferred_ele...]
  transfers between devices with their start and end apart: 4 -> 1, of which waited for: 4 -> 0; matrix products, arithmetic and copies ran while one was open for 1% -> 4% of each run, Pallas kernels for 0% -> 0%
where the time goes in v1:
time: 402 us; the launch traced here: 400 us
  blocking collectives  184 us (46%)
  Pallas kernels  164 us (41%)
  local copies, waits for them, and re-layouts  15.7 us (4%)
  matrix products  14.8 us (4%)
  between operations  13.7 us (3%)
  other arithmetic  7.6 us (2%)
    all_gather x1, blocking collectives, routing(): every = lax.all_gather(both, ('ctx', 'exp'), axis=0, tiled=True)  184 us
    pallas_call x1, Pallas kernels, experts(): pl.pallas_call(experts_kernel, name='experts', out_shape=jax.ShapeDtypeSt...  141 us
    pallas_call x1, Pallas kernels, project(): pl.pallas_call(project_kernel, name='project', out_shape=(jax.ShapeDtypeS...  22.7 us
    dot_general x1, matrix products, attend(): lax.dot_general(query_rows, keys, (((1,), (1,)), ((), ())), preferred_ele...  8.56 us
  transfers between devices with their start and end apart: 1, of which 0 were waited for; matrix products, arithmetic and copies ran while one was open for 4% of the time, Pallas kernels for 0%

profile of v1, /device:TPU:1, one launch (start us, length us, event | category | flops | bytes accessed | tf_op | source)
XLA Modules:
  0.0 399.8 jit_solution(3180697063076865388)
XLA Ops:
  6.5 0.7 all-gather.2.cloned.1.call-update
  7.3 3.8 copy.46
  11.1 2.5 reshape.103
  14.1 183.6 %all_gather.7 = f32[2048,16]{1,0:T(8,128)S(1)} all-gather(f32[16,16]{1,0:T(8,128)S(1)} %copy.50), channel_id=1, replica_groups=mesh['ctx'=8,'exp'=16] {'ctx','exp'}, dimensions={0}, use_global_device_ids=true | all-gather | bytes 132096 | tf_op jit(solution)/shard_map/all_gather | solution.py:621
  197.7 0.3 fusion.27
  198.0 0.3 copy.51
  198.8 4.6 %select_reduce_fusion = s32[2,8,4,2,2,16]{5,4,3,2,1,0:T(2,128)S(1)} fusion(pred[2,8,4,2,2,16]{5,4,3,2,1,0:T(4,128)(4,1)S(1)} %reshape.107, pred[16,16]{1,0:T(8,128)(4,1)S(1)} %iota_compare_fusion.2), kind=kLoop, calls=%fused_computation.8 | loop fusion | flops 192512 | bytes 20736 | tf_op jit(solution)/shard_map/reduce_sum | solution.py:628
  203.5 0.2 reshape.109
  203.9 0.3 copy.55
  204.3 0.2 reshape.110
  204.6 0.8 reshape_reshape.7.weights
  205.5 0.6 add_select_fusion.slots
  206.1 8.6 %fusion.28 = (f32[1536]{0:T(1024)S(1)}, f32[1536,2048]{1,0:T(8,128)S(1)}) fusion(bf16[1536,576]{1,0:T(8,128)(2,1)} %reshape.103, bf16[2048,576]{0,1:T(8,128)(2,1)} %all-gather.2.cloned.1.call-done, s32[1536]{0:T(1024)S(1)} %le.16, s32[2048]{0:T(1024)S(1)} %fusion.23), kind=kOutput, calls=%fused_computation.48 | convolution fusion | flops 3636460032 | bytes 16732160 | tf_op jit(solution)/shard_map/dot_general | solution.py:659
  214.7 1.8 fusion
  216.5 5.1 %divide_convert_fusion = bf16[1536,512]{1,0:T(8,128)(2,1)} fusion(f32[1536,2048]{1,0:T(8,128)S(1)} %get-tuple-element.12, f32[1536]{0:T(1024)S(1)} %get-tuple-element.11, bf16[2048,576]{0,1:T(8,128)(2,1)S(1)} %copy-done.8, f32[1536]{0:T(1024)S(1)} %fusion), kind=kOutput, calls=%fused_computation.6 | convolution fusion | flops 3229089792 | bytes 16269312 | tf_op jit(solution)/shard_map/dot_general | solution.py:663
  221.6 2.5 reshape.104
  224.2 1.1 fusion.13
  225.3 0.3 copy.48
  225.6 0.5 reshape_reshape.6
  226.2 22.7 %project.1 = (f32[8,16,896]{2,1,0:T(8,128)S(1)}, bf16[8,16,896]{2,1,0:T(8,128)(2,1)S(1)}) custom-call(bf16[256,768]{1,0:T(8,128)(2,1)S(1)} %bitcast.11, bf16[768,7168]{1,0:T(8,128)(2,1)} %w_hbm.1, bf16[16,7168]{1,0:T(8,128)(2,1)S(1)} %copy-done.2, f32[1,7168]{1,0:T(1,128)S(1)} %bitcast.12), custom_call_target="tpu_custom_call" | custom-call | tf_op jit(solution)/shard_map/project/pallas_call | solution.py:560
  248.9 0.8 copy-done.1
  249.7 0.7 copy-done.3
  250.4 140.9 %experts.1 = bf16[16,7168]{1,0:T(8,128)(2,1)} custom-call(bf16[8,16,896]{2,1,0:T(8,128)(2,1)} %copy-done.3, s32[8,2,256]{2,1,0:T(2,128)} %add_select_fusion.slots, f32[8,2,256]{2,1,0:T(2,128)} %reshape_reshape.7.weights, f32[8,16,896]{2,1,0:T(8,128)} %copy-done.1, bf16[2,896,2048]{2,1,0:T(8,128)(2,1)} %wg_hbm.1, bf16[2,1024,896]{2,1,0:T(8,128)(2,1)} %wd_hbm.1), custom_call_target="tpu_custom_call" | custom-call | tf_op jit(solution)/shard_map/experts/pallas_call | solution.py:583
  391.3 1.6 copy.66
  (43 shorter events, 1.6 us)
Async XLA Ops:
  6.5 217.6 %copy-start = (bf16[6,512,128]{2,1,0:T(8,128)(2,1)S(1)}, bf16[6,512,128]{2,1,0:T(8,128)(2,1)}, u32[]{:S(2)}) copy-start(bf16[6,512,128]{2,1,0:T(8,128)(2,1)} %param.14) | copy-start | bytes 2359300
  6.5 199.6 %all-gather.2.cloned.1.call-start = ((), (), s32[]{:S(2)}) async-start(), calls=%async_computation | async-start | bytes 2654208 | tf_op jit(solution)/shard_map/all_gather | solution.py:656
  11.0 2.5 copy-start.7
  11.1 2.9 copy-start.5
  11.1 2.9 copy-start.6
  214.7 1.8 copy-start.8
  224.1 2.0 copy-start.2
  224.1 2.0 copy-start.4
  248.9 0.8 copy-start.1
  249.7 0.7 copy-start.3
Sparse Core Ops, SparseCore 0:
  9.5 61.3 all-gather.1

commit v2 on v1

--- a/solution.py
+++ b/solution.py
@@ -165,6 +165,132 @@
     return pl.when(cond)
 
 
+def attend_kernel(scale, queries, latent, query_pos, key_pos, w_uv, routes, out, table,
+                  kb, top, total, value, s_in, r_in, s_c, r_c,
+                  s_tx, r_tx, s_ty, r_ty, s_tc, r_tc, s_tz, r_tz, s_th, r_th):
+    pos = place()
+    z, yh, x, yl, co = pos
+    me = z * 2 + yh
+    core, ylp, xs = exp_peers(pos)
+    yp = dev(z, (yh + 1) % 2, x, yl, co)
+    zs = [dev((z + d) % 4, yh, x, yl, co) for d in (1, 2, 3)]
+    greet([core, ylp] + xs + [dev((z + dz) % 4, (yh + dy) % 2, x, yl, co)
+                              for dz in range(4) for dy in range(2) if dz or dy])
+
+    def c_in(dz, dy):
+        r = dz * 2 + dy
+        return put(latent.at[pl.ds(pl.multiple_of(co * 128, 128), 128)], kb.at[me, co], s_in.at[r], r_in.at[r],
+                   dev((z + dz) % 4, (yh + dy) % 2, x, yl, co))
+
+    def chunk(r):
+        return ((z + 4 - r // 2) % 4) * 2 + (yh + r) % 2
+
+    def c_core(r):
+        c = chunk(r)
+        return put(kb.at[c, co], kb.at[c, co], s_c.at[r], r_c.at[r], core)
+
+    for r in range(1, 8):
+        c_in(r // 2, r % 2).start()
+    kb[me] = latent[...].reshape(kb.shape[1:])
+
+    table[z, yh, co, x, yl] = routes[...]
+
+    def t_x(d):
+        part = table.at[z, yh, co, x, yl]
+        return put(part, part, s_tx.at[d - 1], r_tx.at[d - 1], xs[d - 1])
+
+    def t_z(d):
+        part = table.at[z, yh]
+        return put(part, part, s_tz.at[d - 1], r_tz.at[d - 1], zs[d - 1])
+
+    t_y = put(table.at[z, yh, co, :, yl], table.at[z, yh, co, :, yl], s_ty, r_ty, ylp)
+    t_c = put(table.at[z, yh, co], table.at[z, yh, co], s_tc, r_tc, core)
+    t_h = put(table.at[:, yh], table.at[:, yh], s_th, r_th, yp)
+    for d in (1, 2, 3):
+        t_x(d).start()
+
+    top[...] = jnp.full(top.shape, -1e30, F32)
+    total[...] = jnp.zeros(total.shape, F32)
+    value[...] = jnp.zeros(value.shape, F32)
+    lat_width = value.shape[2]
+
+    def attend_chunk(r):
+        c = chunk(r)
+
+        def head(h):
+            keys = kb[c].reshape(256, kb.shape[3])
+            s = lax.dot_general(queries[h], keys, (((1,), (1,)), ((), ())), preferred_element_type=F32)
+            s = jnp.where(key_pos[c] <= query_pos[...], s, -jnp.inf)
+            old = top[h, :, :1]
+            new = jnp.maximum(old, jnp.max(s, axis=1, keepdims=True))
+            p = jnp.exp2((s - new) * scale)
+            fade = jnp.exp2((old - new) * scale)
+            top[h] = jnp.broadcast_to(new, top.shape[1:])
+            total[h] = total[h] * fade + jnp.sum(p, axis=1, keepdims=True)
+            value[h] = value[h] * fade + jnp.dot(p.astype(BF), keys[:, :lat_width], preferred_element_type=F32)
+
+        loop(queries.shape[0], head)
+
+    def step(k):
+        @when(k < 7)
+        def _():
+            for r in range(1, 8):
+                @when(k + 1 == r)
+                def _():
+                    c_in(r // 2, r % 2).wait_recv()
+            c_core(k + 1).start()
+
+        @when(k == 1)
+        def _():
+            for d in (1, 2, 3):
+                t_x(d).wait_recv()
+            t_y.start()
+
+        @when(k == 2)
+        def _():
+            t_y.wait_recv()
+            t_c.start()
+
+        @when(k == 3)
+        def _():
+            t_c.wait_recv()
+            for d in (1, 2, 3):
+                t_z(d).start()
+
+        @when(k == 4)
+        def _():
+            for d in (1, 2, 3):
+                t_z(d).wait_recv()
+            t_h.start()
+
+        @when(k > 0)
+        def _():
+            c_core(k).wait_recv()
+
+        attend_chunk(k)
+
+    loop(8, step)
+
+    def finish(h):
+        context = (value[h] / total[h, :, :1]).astype(BF)
+        r = jnp.dot(context, w_uv[h], preferred_element_type=F32).astype(BF)
+        cols = pl.ds(pl.multiple_of(h * 128, 128), 128)
+        for half in range(2):
+            out[pl.ds(pl.multiple_of((half + co + 1) % 2 * 128, 128), 128), cols] = r[half * 128:half * 128 + 128]
+
+    loop(queries.shape[0], finish)
+    t_h.wait_recv()
+    for r in range(1, 8):
+        c_in(r // 2, r % 2).wait_send()
+        c_core(r).wait_send()
+    for d in (1, 2, 3):
+        t_x(d).wait_send()
+        t_z(d).wait_send()
+    t_y.wait_send()
+    t_c.wait_send()
+    t_h.wait_send()
+
+
 def project_kernel(heads, w_hbm, resid, gain, state, normed, w, wsem, *reduce_refs):
     pos = place()
     core, ylp, xs = exp_peers(pos)
@@ -215,8 +341,8 @@
     loop(4, red.drain)
 
 
-def experts_kernel(normed, slots, weights, state, wg_hbm, wd_hbm, out,
-                   wg, wd, wsem, xb, rows, abuf, la, bbuf, bown, lb1, b2, lb2, a2, la2, suma,
+def experts_kernel(normed, table, state, wg_hbm, wd_hbm, out,
+                   slots, weights, hits, wg, wd, wsem, xb, rows, abuf, la, bbuf, bown, lb1, b2, lb2, a2, la2, suma,
                    acta, actb, yrow, tbuf, fin, ret, sems, *reduce_refs):
     pos = place()
     z, yh, x, yl, co = pos
@@ -309,7 +435,23 @@
     def c_b2(dz):
         return put(b2.at[dz], lb2.at[dz], s_b2.at[dz], r_b2.at[dz], dev((z + 4 - dz) % 4, yh, x, yl, co))
 
-    row_id = lax.broadcasted_iota(jnp.int32, (96, 256), 0)
+    def find(k):
+        for i in range(2):
+            mine = table[k, :8, :] == (lax.axis_index("exp") * 2 + i).astype(F32)
+            hits[k, i:i + 1, :] = jnp.max(jnp.where(mine, 1.0, 0.0), axis=0, keepdims=True)
+            weights[k, i:i + 1, :] = jnp.sum(jnp.where(mine, table[k, 8:, :], 0.0), axis=0, keepdims=True)
+
+    loop(8, find)
+    one, two = (lax.broadcasted_iota(jnp.int32, (256, 256), a) for a in (0, 1))
+    before = jnp.where((one < two) & (one // 16 == two // 16), 1.0, 0.0).astype(BF)
+    block = (lax.broadcasted_iota(jnp.int32, (2, 256), 1) // 16 * 6).astype(F32)
+
+    def rank(k):
+        r = jnp.dot(hits[k].astype(BF), before, preferred_element_type=F32)
+        slots[k] = jnp.where(hits[k] > 0.5, block + r, -1.0)
+
+    loop(8, rank)
+    row_id = lax.broadcasted_iota(jnp.int32, (96, 256), 0).astype(F32)
 
     def gate_up(dz):
         for dy in range(2):
@@ -569,7 +711,7 @@
     )(heads, w_out, resid, gain)
 
 
-def experts(normed, slots, weights, state, w_gate_up, w_down):
+def experts(normed, table, state, w_gate_up, w_down):
     hid2 = w_gate_up.shape[2]
     hid = hid2 // 2
     sems = [
@@ -584,9 +726,12 @@
         experts_kernel,
         name="experts",
         out_shape=jax.ShapeDtypeStruct((16, 8 * W), BF),
-        in_specs=[VM, VM, VM, VM, ANY, ANY],
+        in_specs=[VM, VM, VM, ANY, ANY],
         out_specs=VM,
         scratch_shapes=[
+            pltpu.VMEM((8, 2, 256), F32),
+            pltpu.VMEM((8, 2, 256), F32),
+            pltpu.VMEM((8, 2, 256), F32),
             pltpu.VMEM((2, W, hid2), BF),
             pltpu.VMEM((2, hid, W), BF),
             DMA((3,)),
@@ -612,68 +757,53 @@
         ] + REDUCE_SCRATCH,
         compiler_params=pltpu.CompilerParams(
             collective_id=2, has_side_effects=True, vmem_limit_bytes=62 << 20),
-    )(normed, slots, weights, state, w_gate_up, w_down)
-
-
-def routing(expert_ids, route_weights):
-    e = lax.axis_index("exp")
-    both = jnp.concatenate([expert_ids.astype(F32), route_weights], axis=1)
-    every = lax.all_gather(both, ("ctx", "exp"), axis=0, tiled=True)
-    mine = (2 * e + jnp.arange(2)).astype(F32)
-    match = every[None, :, :8] == mine[:, None, None]
-    hit = jnp.any(match, axis=2)
-    weight = jnp.sum(jnp.where(match, every[None, :, 8:], 0.0), axis=2)
-    hit = hit.reshape(2, 8, 4, 2, 2, 16)
-    before = jnp.arange(16)[:, None] > jnp.arange(16)[None, :]
-    rank = jnp.sum(jnp.where(before & hit[..., None, :], 1, 0), axis=-1)
-    hit, rank, weight = (
-        jnp.transpose(t.reshape(2, 8, 4, 2, 2, 16), (1, 0, 4, 2, 3, 5)).reshape(8, 2, 16, 16)
-        for t in (hit, rank, weight)
-    )
-    slot = jnp.where(hit, jnp.arange(16)[:, None] * 6 + rank, -1)
-    return slot.reshape(8, 2, 256).astype(jnp.int32), weight.reshape(8, 2, 256)
-
-
-def attend(queries, latent, block_order, w_uv):
-    query_count, heads_dev, feat_width = queries.shape
-    lat_width = w_uv.shape[1]
-    value_width = w_uv.shape[2]
-    block_len = query_count // 2
-    stored_blocks = block_order.shape[0]
+    )(normed, table, state, w_gate_up, w_down)
+
+
+def attend(queries, latent, query_pos, key_pos, w_uv, routes):
+    heads_dev, query_count, feat_width = queries.shape
+    lat_width, value_width = w_uv.shape[1:]
     score_scale = (value_width + feat_width - lat_width) ** (-0.5)
-    ctx_rank = lax.axis_index("ctx")
-
-    def seq_positions(first_row, count):
-        row_ids = first_row + jnp.arange(count, dtype=jnp.int32)
-        block_ids = row_ids // block_len
-        match = block_ids[:, None] == jnp.arange(stored_blocks, dtype=jnp.int32)[None, :]
-        block_pos = jnp.sum(jnp.where(match, block_order[None, :], 0), axis=1)
-        return block_pos * block_len + row_ids % block_len
-
-    query_pos = seq_positions(ctx_rank * query_count, query_count)
-    query_rows = queries.reshape(query_count * heads_dev, feat_width)
-    query_pos_rows = jnp.repeat(query_pos, heads_dev)
-    keys = lax.all_gather(latent, "ctx", axis=0, tiled=True)
-    key_pos = seq_positions(jnp.int32(0), keys.shape[0])
-    scores = (
-        lax.dot_general(query_rows, keys, (((1,), (1,)), ((), ())), preferred_element_type=F32) * score_scale
-    )
-    scores = jnp.where(key_pos[None, :] <= query_pos_rows[:, None], scores, -jnp.inf)
-    weights = jnp.exp(scores - jnp.max(scores, axis=1)[:, None])
-    value_sum = jnp.dot(weights.astype(BF), keys[:, :lat_width], preferred_element_type=F32)
-    weight_sum = jnp.sum(weights, axis=1)
-    context = (value_sum / weight_sum[:, None]).astype(BF).reshape(query_count, heads_dev, lat_width)
-    head_out = jnp.einsum("shl,hlv->shv", context, w_uv, preferred_element_type=F32).astype(BF)
-    return head_out.reshape(query_count, heads_dev * value_width)
+    return pl.pallas_call(
+        functools.partial(attend_kernel, score_scale * 1.4426950408889634),
+        name="attend",
+        out_shape=(
+            jax.ShapeDtypeStruct((query_count, heads_dev * value_width), BF),
+            jax.ShapeDtypeStruct((4, 2, 2, 4, 2, 16, 16), F32),
+        ),
+        in_specs=[VM] * 6,
+        out_specs=(VM, VM),
+        scratch_shapes=[
+            pltpu.VMEM((8, 2, 128, feat_width), BF),
+            pltpu.VMEM((heads_dev, query_count, 128), F32),
+            pltpu.VMEM((heads_dev, query_count, 128), F32),
+            pltpu.VMEM((heads_dev, query_count, lat_width), F32),
+            DMA((8,)), DMA((8,)), DMA((8,)), DMA((8,)),
+            DMA((3,)), DMA((3,)), DMA, DMA, DMA, DMA, DMA((3,)), DMA((3,)), DMA, DMA,
+        ],
+        compiler_params=pltpu.CompilerParams(
+            collective_id=3, has_side_effects=True, vmem_limit_bytes=40 << 20),
+    )(queries, latent, query_pos, key_pos, w_uv, routes)
+
+
+def positions(block_order):
+    return (block_order[:, None] * 128 + jnp.arange(128, dtype=jnp.int32)[None, :]).reshape(8, 256)
 
 
 def body(queries, latent, block_order, w_uv, w_out, resid, norm_gain, expert_ids, route_weights, w_gate_up, w_down):
-    slots, weights = routing(expert_ids, route_weights)
-    head_out = attend(queries, latent, block_order, w_uv)
-    by_core = head_out.reshape(8, 2, 16, -1).transpose(1, 0, 2, 3)
-    by_core = jnp.where(lax.axis_index("exp") % 2 == 0, by_core[::-1], by_core).reshape(256, -1)
-    state, normed = project(by_core, w_out, resid, norm_gain.reshape(1, -1))
-    return experts(normed, slots, weights, state, w_gate_up, w_down)
+    def by_core(t, axis):
+        shape = t.shape
+        t = t.reshape(shape[:axis] + (8, 2, 16) + shape[axis + 1:])
+        return jnp.swapaxes(t, axis, axis + 1).reshape(shape)
+
+    pos = positions(block_order)
+    mine = lax.dynamic_index_in_dim(pos, lax.axis_index("ctx"), 0, keepdims=False)
+    routes = jnp.concatenate([expert_ids.astype(F32), route_weights], axis=1).T
+    head_out, table = attend(
+        by_core(queries, 0).transpose(1, 0, 2), latent, by_core(mine, 0)[:, None], pos[:, None, :], w_uv, routes)
+    table = table.reshape(8, 16, 16, 16).transpose(0, 2, 1, 3).reshape(8, 16, 256)
+    state, normed = project(head_out, w_out, resid, norm_gain.reshape(1, -1))
+    return experts(normed, table, state, w_gate_up, w_down)
 
 
 def solution(mesh):

time: 402 us -> 238 us (0.59)
  blocking collectives: 184 us -> 0 us
  Pallas kernels: 164 us -> 224 us
  matrix products: 14.8 us -> 0 us
  between operations: 13.7 us -> 0.17 us
  other arithmetic: 7.6 us -> 0.05 us
  local copies, waits for them, and re-layouts: 15.7 us -> 10.9 us
    all_gather x1 -> x0, blocking collectives: 184 us -> none  [routing(): every = lax.all_gather(both, ('ctx', 'exp'), axis=0, tiled=True)]
    pallas_call x0 -> x1, Pallas kernels: none -> 54.1 us  [attend(): pl.pallas_call(functools.partial(attend_kernel, score_scale * 1.442695040...]
    dot_general x3 -> x0, matrix products: 14.8 us -> none  [the longest x1 8.56 us: attend(): lax.dot_general(query_rows, keys, (((1,), (1,)), ((), ())), preferred_ele...]
    reduce_sum x5 -> x0, other arithmetic: 6.72 us -> none  [the longest x1 4.6 us: routing(): rank = jnp.sum(jnp.where(before & hit[..., None, :], 1, 0), axis=-1)]
    pallas_call x1, Pallas kernels: 22.7 us -> 27.3 us  [project(): pl.pallas_call(project_kernel, name='project', out_shape=(jax.ShapeDtypeS...]
    reshape x7 -> x3, local copies, waits for them, and re-layouts: 5.71 us -> 1.46 us  [the longest x2 1.37 us: body(): table.reshape(8, 16, 16, 16).transpose(0, 2, 1, 3).reshape(8, 16, 256)]
  transfers between devices with their start and end apart: 1 -> 0, of which waited for: 0 -> 0; matrix products, arithmetic and copies ran while one was open for 4% -> 0% of each run, Pallas kernels for 0% -> 0%
where the time goes in v2:
time: 238 us; the launch traced here: 235 us
  Pallas kernels  224 us (94%)
  local copies, waits for them, and re-layouts  10.9 us (5%)
    pallas_call x1, Pallas kernels, experts(): pl.pallas_call(experts_kernel, name='experts', out_shape=jax.ShapeDtypeSt...  143 us
    pallas_call x1, Pallas kernels, attend(): pl.pallas_call(functools.partial(attend_kernel, score_scale * 1.442695040...  54.1 us
    pallas_call x1, Pallas kernels, project(): pl.pallas_call(project_kernel, name='project', out_shape=(jax.ShapeDtypeS...  27.3 us
    unnamed x21, local copies, waits for them, and re-layouts  7.41 us

profile of v2, /device:TPU:1, one launch (start us, length us, event | category | flops | bytes accessed | tf_op | source)
XLA Modules:
  0.0 235.5 jit_solution(1625746526995802405)
XLA Ops:
  0.0 0.0 copy-start.5
  0.0 4.0 %copy.15 = bf16[256,6,576]{2,0,1:T(8,128)(2,1)} copy(bf16[256,6,576]{0,2,1:T(8,128)(2,1)} %param.11) | data formatting | bytes 3538944 | tf_op args[0]
  4.0 1.8 copy.16
  5.9 1.2 copy.18.latent
  7.0 0.0 copy-done.7
  7.0 0.1 add.43
  7.1 0.1 broadcast_bitcast_fusion
  7.2 0.1 reshape.66
  7.3 0.1 broadcast_in_dim_reshape.5.query_pos
  7.4 0.1 add.44
  7.5 0.0 copy-done.5
  7.6 0.0 copy-done.6
  7.6 0.0 copy-done
  7.6 54.1 %attend.1 = (bf16[256,768]{1,0:T(8,128)(2,1)S(1)}, f32[4,2,2,4,2,16,16]{6,5,4,3,2,1,0:T(8,128)S(1)}) custom-call(bf16[6,256,576]{2,1,0:T(8,128)(2,1)S(1)} %bitcast.24, bf16[256,576]{1,0:T(8,128)(2,1)S(1)} %copy.18.latent, s32[256,1]{1,0:T(8,128)S(1)} %broadcast_in_dim_reshape.5.query_pos, s32[8,1,256]{2,1,0:T(1,128)S(1)} %broadcast_add_fusion.key_pos, ...), custom_call_target="tpu_custom_call" | custom-call | tf_op jit(solution)/shard_map/attend/pallas_call | solution.py:767
  61.7 0.0 copy-done.2
  61.7 0.0 copy-done.4
  61.7 27.3 %project.1 = (f32[8,16,896]{2,1,0:T(8,128)S(1)}, bf16[8,16,896]{2,1,0:T(8,128)(2,1)S(1)}) custom-call(bf16[256,768]{1,0:T(8,128)(2,1)S(1)} %get-tuple-element.9.heads, bf16[768,7168]{1,0:T(8,128)(2,1)} %w_hbm.1, bf16[16,7168]{1,0:T(8,128)(2,1)S(1)} %copy-done.2, f32[1,7168]{1,0:T(1,128)S(1)} %bitcast.26), custom_call_target="tpu_custom_call" | custom-call | tf_op jit(solution)/shard_map/project/pallas_call | solution.py:702
  89.0 0.0 copy-start.3
  89.0 0.3 copy.24
  89.4 0.4 copy-done.1
  89.8 0.1 copy-done.3
  89.9 1.1 reshape.69.table
  90.9 142.9 %experts.1 = bf16[16,7168]{1,0:T(8,128)(2,1)} custom-call(bf16[8,16,896]{2,1,0:T(8,128)(2,1)} %copy-done.3, f32[8,16,256]{2,1,0:T(8,128)} %reshape.69.table, f32[8,16,896]{2,1,0:T(8,128)} %copy-done.1, bf16[2,896,2048]{2,1,0:T(8,128)(2,1)} %wg_hbm.1, bf16[2,1024,896]{2,1,0:T(8,128)(2,1)} %wd_hbm.1), custom_call_target="tpu_custom_call" | custom-call | tf_op jit(solution)/shard_map/experts/pallas_call | solution.py:725
  233.9 1.6 copy.27
  (14 shorter events, 0.1 us)
Async XLA Ops:
  0.0 7.0 %copy-start.7 = (s32[16]{0:T(128)S(1)}, s32[16]{0:T(128)}, u32[]{:S(2)}) copy-start(s32[16]{0:T(128)} %param.13) | copy-start | bytes 196
  0.0 7.6 %copy-start = (bf16[6,512,128]{2,1,0:T(8,128)(2,1)S(1)}, bf16[6,512,128]{2,1,0:T(8,128)(2,1)}, u32[]{:S(2)}) copy-start(bf16[6,512,128]{2,1,0:T(8,128)(2,1)} %w_uv.1) | copy-start | bytes 2359300
  0.0 7.6 %copy-start.6 = (f32[16,8]{0,1:T(8,128)S(1)}, f32[16,8]{0,1:T(8,128)}, u32[]{:S(2)}) copy-start(f32[16,8]{0,1:T(8,128)} %param.19) | copy-start | bytes 1540
  0.0 7.5 %copy-start.5 = (s32[16,8]{0,1:T(8,128)S(1)}, s32[16,8]{0,1:T(8,128)}, u32[]{:S(2)}) copy-start(s32[16,8]{0,1:T(8,128)} %param.18) | copy-start | bytes 1540
  4.0 57.7 %copy-start.2 = (bf16[16,7168]{1,0:T(8,128)(2,1)S(1)}, bf16[16,7168]{1,0:T(8,128)(2,1)}, u32[]{:S(2)}) copy-start(bf16[16,7168]{1,0:T(8,128)(2,1)} %resid.1) | copy-start | bytes 688132
  4.0 57.7 %copy-start.4 = (f32[7168]{0:T(1024)S(1)}, f32[7168]{0:T(1024)}, u32[]{:S(2)}) copy-start(f32[7168]{0:T(1024)} %param.17) | copy-start | bytes 86020
  89.0 0.8 copy-start.1
  89.0 0.8 copy-start.3

commit v3 on v2

v3 whole, which is shorter than its diff:
```python
import functools

import jax
import jax.numpy as jnp
from jax import lax
from jax.experimental import pallas as pl
from jax.experimental.pallas import tpu as pltpu
from jax.sharding import PartitionSpec as P

BF = jnp.bfloat16
F32 = jnp.float32
DMA = pltpu.SemaphoreType.DMA
W = 896


def place():
    c = lax.axis_index("ctx")
    e = lax.axis_index("exp")
    return c // 2, c % 2, e // 4, (e // 2) % 2, e % 2


def dev(z, yh, x, yl, co):
    return (z * 2 + yh, x * 4 + yl * 2 + co)


def put(src, dst, ss, rs, device):
    return pltpu.make_async_remote_copy(
        src_ref=src,
        dst_ref=dst,
        send_sem=ss,
        recv_sem=rs,
        device_id=device,
        device_id_type=pl.DeviceIdType.MESH,
    )


def greet(devices):
    barrier = pltpu.get_barrier_semaphore()
    for d in devices:
        pl.semaphore_signal(barrier, inc=1, device_id=d, device_id_type=pl.DeviceIdType.MESH)
    pl.semaphore_wait(barrier, len(devices))


def exp_peers(pos):
    z, yh, x, yl, co = pos
    core = dev(z, yh, x, yl, (co + 1) % 2)
    ylp = dev(z, yh, x, (yl + 1) % 2, co)
    xs = [dev(z, yh, (x + d) % 4, yl, co) for d in (1, 2, 3)]
    return core, ylp, xs


REDUCE_SCRATCH = [
    pltpu.VMEM((8, 4, 2, 16, W), F32),
    pltpu.VMEM((8, 4, 2, 16, W), BF),
    pltpu.VMEM((8, 4, 2, 16, W), BF),
    pltpu.VMEM((8, 4, 2, 16, W), BF),
    pltpu.VMEM((4, 3, 2, 16, W), BF),
    pltpu.VMEM((8, 4, 16, W), BF),
    pltpu.VMEM((4, 16, W), BF),
    pltpu.VMEM((8, 3, 16, W), BF),
    pltpu.VMEM((4, 16, W), BF),
    pltpu.VMEM((8, 3, 16, W), BF),
    pltpu.VMEM((8, 16, W), F32),
    DMA((8,)),
    DMA((8,)),
    DMA((4, 3)),
    DMA((4, 3)),
    DMA((8,)),
    DMA((8,)),
    DMA((4,)),
    DMA((4,)),
    DMA((8, 3)),
    DMA((8, 3)),
]


class Reduce:
    def __init__(self, refs, pos, crossed):
        (self.own, self.cs, self.cl, self.s1, self.x1, self.y1, self.y2s, self.x2s, self.y2,
         self.x2, self.acc, *self.sems) = refs
        self.pos = pos
        self.crossed = crossed
        self.core, self.ylp, self.xs = exp_peers(pos)

    def c_core(self, n):
        return put(self.cs.at[n], self.cl.at[n], self.sems[0].at[n], self.sems[1].at[n], self.core)

    def c_x1(self, i, d):
        xx = (self.pos[2] + d) % 4
        return put(self.s1.at[2 * i, xx], self.x1.at[i, d - 1], self.sems[2].at[i, d - 1],
                   self.sems[3].at[i, d - 1], self.xs[d - 1])

    def c_y1(self, n):
        return put(self.s1.at[n, :, (self.pos[3] + 1) % 2], self.y1.at[n], self.sems[4].at[n],
                   self.sems[5].at[n], self.ylp)

    def c_y2(self, i):
        return put(self.y2s.at[i], self.y2.at[i], self.sems[6].at[i], self.sems[7].at[i], self.ylp)

    def c_x2(self, n, part, odd):
        plus = (part == 1) == odd
        return put(self.x2s.at[n, part], self.x2.at[n, part], self.sems[8].at[n, part],
                   self.sems[9].at[n, part], self.xs[0 if plus else 2])

    def over_y(self, n, xx):
        return self.s1[n, xx, self.pos[3]].astype(F32) + self.y1[n, xx].astype(F32)

    def first(self, i):
        for j in range(2):
            n = 2 * i + j
            self.c_core(n).wait_recv()
            self.s1[n] = (self.own[n] + self.cl[n].astype(F32)).astype(BF)
            if self.crossed and j == 0:
                for d in (1, 2, 3):
                    self.c_x1(i, d).start()
            else:
                self.c_y1(n).start()

    def second(self, i):
        x, yl = self.pos[2], self.pos[3]
        for j in range(2):
            n = 2 * i + j
            if self.crossed and j == 0:
                for d in (1, 2, 3):
                    self.c_x1(i, d).wait_recv()

                def over_x(which):
                    t = self.s1[n, x, which].astype(F32)
                    for d in (0, 1, 2):
                        t = t + self.x1[i, d, which].astype(F32)
                    return t

                self.y2s[i] = over_x((yl + 1) % 2).astype(BF)
                self.c_y2(i).start()
                self.acc[n] = over_x(yl)
            else:
                self.c_y1(n).wait_recv()
                for part, d in ((0, 2), (1, 1 if j else 3)):
                    self.x2s[n, part] = self.over_y(n, (x + d) % 4).astype(BF)
                    self.c_x2(n, part, j == 1).start()
                self.acc[n] = self.over_y(n, x)

    def carry(self, i):
        for j in range(2):
            n = 2 * i + j
            if not (self.crossed and j == 0):
                self.c_x2(n, 0, j == 1).wait_recv()
                xx = (self.pos[2] + (3 if j else 1)) % 4
                self.x2s[n, 2] = (self.over_y(n, xx) + self.x2[n, 0].astype(F32)).astype(BF)
                self.c_x2(n, 2, j == 1).start()

    def third(self, i):
        for j in range(2):
            n = 2 * i + j
            t = self.acc[n]
            if self.crossed and j == 0:
                self.c_y2(i).wait_recv()
                t = t + self.y2[i].astype(F32)
            else:
                for part in (1, 2):
                    self.c_x2(n, part, j == 1).wait_recv()
                    t = t + self.x2[n, part].astype(F32)
            self.acc[n] = t

    def drain(self, i):
        for j in range(2):
            n = 2 * i + j
            self.c_core(n).wait_send()
            if self.crossed and j == 0:
                self.c_y2(i).wait_send()
            else:
                self.c_y1(n).wait_send()
            for d in (1, 2, 3):
                if self.crossed and j == 0:
                    self.c_x1(i, d).wait_send()
                else:
                    self.c_x2(n, d - 1, j == 1).wait_send()


REDUCE_X_SCRATCH = [
    pltpu.VMEM((8, 4, 2, 16, W), F32),
    pltpu.VMEM((8, 4, 2, 16, W), BF),
    pltpu.VMEM((8, 4, 2, 16, W), BF),
    pltpu.VMEM((8, 4, 2, 16, W), BF),
    pltpu.VMEM((8, 2, 16, W), BF),
    pltpu.VMEM((8, 3, 2, 16, W), BF),
    pltpu.VMEM((8, 16, W), BF),
    pltpu.VMEM((8, 16, W), BF),
    pltpu.VMEM((8, 16, W), F32),
    DMA((8,)),
    DMA((8,)),
    DMA((8, 3)),
    DMA((8, 3)),
    DMA((8,)),
    DMA((8,)),
]


class ReduceX:
    def __init__(self, refs, pos):
        (self.own, self.cs, self.cl, self.s1, self.xc, self.xl, self.ys, self.yr, self.acc, *self.sems) = refs
        self.pos = pos
        self.core, self.ylp, self.xs = exp_peers(pos)

    def c_core(self, n):
        return put(self.cs.at[n], self.cl.at[n], self.sems[0].at[n], self.sems[1].at[n], self.core)

    def c_x(self, n, part, odd):
        x = self.pos[2]
        if part == 2:
            src = self.xc.at[n]
        else:
            src = self.s1.at[n, (x + 2) % 4 if part == 0 else (x + (1 if odd else 3)) % 4]
        plus = (part == 1) == odd
        return put(src, self.xl.at[n, part], self.sems[2].at[n, part], self.sems[3].at[n, part],
                   self.xs[0 if plus else 2])

    def c_y(self, n):
        return put(self.ys.at[n], self.yr.at[n], self.sems[4].at[n], self.sems[5].at[n], self.ylp)

    def first(self, i):
        for j in range(2):
            n = 2 * i + j
            self.c_core(n).wait_recv()
            self.s1[n] = (self.own[n] + self.cl[n].astype(F32)).astype(BF)
            self.c_x(n, 0, j == 1).start()
            self.c_x(n, 1, j == 1).start()

    def second(self, i):
        for j in range(2):
            n = 2 * i + j
            self.c_x(n, 0, j == 1).wait_recv()
            near = (self.pos[2] + (3 if j else 1)) % 4
            self.xc[n] = (self.s1[n, near].astype(F32) + self.xl[n, 0].astype(F32)).astype(BF)
            self.c_x(n, 2, j == 1).start()

    def carry(self, i):
        x, yl = self.pos[2], self.pos[3]
        for j in range(2):
            n = 2 * i + j
            self.c_x(n, 1, j == 1).wait_recv()
            self.c_x(n, 2, j == 1).wait_recv()

            def over_x(which):
                t = self.s1[n, x, which].astype(F32)
                return t + self.xl[n, 1, which].astype(F32) + self.xl[n, 2, which].astype(F32)

            self.ys[n] = over_x((yl + 1) % 2).astype(BF)
            self.c_y(n).start()
            self.acc[n] = over_x(yl)

    def third(self, i):
        for j in range(2):
            n = 2 * i + j
            self.c_y(n).wait_recv()
            self.acc[n] = self.acc[n] + self.yr[n].astype(F32)

    def drain(self, i):
        for j in range(2):
            n = 2 * i + j
            self.c_core(n).wait_send()
            self.c_y(n).wait_send()
            for part in range(3):
                self.c_x(n, part, j == 1).wait_send()


def loop(count, step):
    def body(k, carry):
        step(k)
        return carry

    lax.fori_loop(0, count, body, 0)


def when(cond):
    return pl.when(cond)


def attend_kernel(scale, block_order, queries, latent, w_uv, ids, weights, out, table,
                  kb, near, qs, top, scores, mid, part, some,
                  s_a, r_a, s_ay, r_ay, s_b, r_b, s_by, r_by, s_c, r_c,
                  s_tx, r_tx, s_ty, r_ty, s_tc, r_tc, s_tz, r_tz, s_th, r_th):
    pos = place()
    z, yh, x, yl, co = pos
    core, ylp, xs = exp_peers(pos)
    yp = dev(z, (yh + 1) % 2, x, yl, co)
    zs = [dev((z + d) % 4, yh, x, yl, co) for d in (1, 2, 3)]
    above, below = zs[0], zs[2]
    feat = latent.shape[0]
    heads = queries.shape[0]
    lat_width = w_uv.shape[1]
    greet([core, ylp, yp] + xs + zs)

    def c_a(p):
        plane, first, count = ((0, 0, 64), (0, 0, 64), (1, 0, 32), (3, 32, 32))[p]
        src = kb.at[(z + plane) % 4, yh, co, pl.ds(first, count)]
        return put(src, src, s_a.at[p], r_a.at[p], above if p in (0, 3) else below)

    def c_ay(dz):
        src = kb.at[(z + 4 - dz) % 4, yh, co, pl.ds(0, 64)]
        return put(src, src, s_ay.at[dz], r_ay.at[dz], yp)

    def c_b(p):
        if p < 2:
            src = kb.at[z, :, co, pl.ds(64, 64)]
        elif p == 2:
            src = kb.at[(z + 1) % 4, 0, co, pl.ds(64, 64)]
        else:
            src = kb.at[(z + 3) % 4, 1, co, pl.ds(64, 64)]
        return put(src, src, s_b.at[p], r_b.at[p], above if p in (0, 3) else below)

    own = kb.at[z, yh, co, pl.ds(64, 64)]
    c_by = put(own, own, s_by, r_by, yp)

    def c_core(dz, dy):
        src = kb.at[(z + 4 - dz) % 4, (yh + dy) % 2, co]
        return put(src, src, s_c.at[dz, dy], r_c.at[dz, dy], core)

    kb[z, yh, :, :, feat:] = jnp.zeros((2, 128, kb.shape[4] - feat), BF)
    kb[z, yh, :, :, :feat] = latent[...].T.reshape(2, 128, feat)
    c_a(0).start()
    c_a(1).start()
    c_by.start()
    c_ay(0).start()

    near[co, x, yl] = jnp.zeros((16, 128), BF)
    near[co, x, yl, :, :16] = jnp.concatenate([ids[...].astype(F32), weights[...]], axis=0).astype(BF)

    def t_x(d):
        src = near.at[co, x, yl]
        return put(src, src, s_tx.at[d - 1], r_tx.at[d - 1], xs[d - 1])

    def t_z(d):
        src = table.at[z, yh]
        return put(src, src, s_tz.at[d - 1], r_tz.at[d - 1], zs[d - 1])

    t_y = put(near.at[co, :, yl], near.at[co, :, yl], s_ty, r_ty, ylp)
    t_c = put(near.at[co], near.at[co], s_tc, r_tc, core)
    t_h = put(table.at[:, yh], table.at[:, yh], s_th, r_th, yp)
    for d in (1, 2, 3):
        t_x(d).start()

    def pack():
        row = lax.broadcasted_iota(jnp.int32, (128, 256), 0)
        col = lax.broadcasted_iota(jnp.int32, (128, 256), 1)
        t = jnp.zeros((16, 256), F32)
        for i in range(16):
            move = jnp.where((col - row == 16 * i) & (row < 16), 1.0, 0.0).astype(BF)
            t = t + jnp.dot(near[i // 8, i // 2 % 4, i % 2], move, preferred_element_type=F32)
        table[z, yh] = t

    def turn(h):
        qs[h] = queries[h].T

    loop(heads, turn)
    top[...] = jnp.full(top.shape, -jnp.inf, F32)

    def place_of(c, axis):
        shape = (1, 256) if axis else (256, 1)
        at = lax.broadcasted_iota(jnp.int32, shape, axis)
        return jnp.where(at < 128, block_order[2 * c] * 128 + at, block_order[2 * c + 1] * 128 + (at - 128))

    def attend_chunk(r):
        zz, yy = (z + 4 - r // 2) % 4, (yh + r) % 2
        hidden = jnp.where(place_of(zz * 2 + yy, 1) <= place_of(z * 2 + yh, 0), 0.0, -jnp.inf)
        keys = kb[zz, yy].reshape(256, kb.shape[4])[:, :feat]
        for h in range(heads):
            s = lax.dot_general(qs[h], keys, (((1,), (1,)), ((), ())), preferred_element_type=F32)
            s = s + hidden
            scores[r, h] = s
            top[h] = jnp.maximum(top[h], jnp.maximum(s[:, :128], s[:, 128:]))

    def weigh(h, most, chunks):
        total = jnp.zeros((256, 128), F32)
        value = jnp.zeros((256, lat_width), F32)
        for r in chunks:
            p = jnp.exp2((scores[r, h] - most) * scale)
            total = total + (p[:, :128] + p[:, 128:])
            keys = kb[(z + 4 - r // 2) % 4, (yh + r) % 2].reshape(256, kb.shape[4])[:, :lat_width]
            value = value + jnp.dot(p.astype(BF), keys, preferred_element_type=F32)
        return total, value

    early, late = (0, 1, 2, 6), (3, 7, 4, 5)

    def begin(h):
        most = jnp.max(top[h], axis=1, keepdims=True)
        mid[h] = jnp.broadcast_to(most, mid.shape[1:])
        part[h], some[h] = weigh(h, most, early)

    def finish(h):
        most = jnp.max(top[h], axis=1, keepdims=True)
        fade = jnp.exp2((mid[h, :, :1] - most) * scale)
        total, value = weigh(h, most, late)
        total = jnp.sum(total + part[h] * fade, axis=1, keepdims=True)
        context = ((value + some[h] * fade) / total).astype(BF)
        r = jnp.dot(context, w_uv[h], preferred_element_type=F32).astype(BF)
        cols = pl.ds(pl.multiple_of(h * 128, 128), 128)
        for g in range(16):
            row = (g % 2 + co + 1) % 2 * 128 + g // 2 * 16
            out[pl.ds(pl.multiple_of(row, 16), 16), cols] = r[g * 16:g * 16 + 16]

    attend_chunk(0)
    c_by.wait_recv()
    c_b(0).start()
    c_b(1).start()
    c_ay(0).wait_recv()
    c_core(0, 1).start()
    c_a(0).wait_recv()
    c_a(3).start()
    c_ay(1).start()
    c_a(1).wait_recv()
    c_a(2).start()
    c_ay(3).start()
    for d in (1, 2, 3):
        t_x(d).wait_recv()
    t_y.start()
    c_core(0, 1).wait_recv()
    attend_chunk(1)
    c_b(0).wait_recv()
    c_b(3).start()
    c_core(1, 0).start()
    c_b(1).wait_recv()
    c_b(2).start()
    c_core(3, 0).start()
    c_a(2).wait_recv()
    c_a(3).wait_recv()
    c_ay(2).start()
    t_y.wait_recv()
    t_c.start()
    c_core(1, 0).wait_recv()
    attend_chunk(2)
    c_ay(1).wait_recv()
    c_core(1, 1).start()
    c_ay(3).wait_recv()
    c_core(3, 1).start()
    c_core(3, 0).wait_recv()
    attend_chunk(6)
    t_c.wait_recv()
    pack()
    for d in (1, 2, 3):
        t_z(d).start()
    loop(heads, begin)
    c_b(2).wait_recv()
    c_b(3).wait_recv()
    c_core(2, 0).start()
    c_ay(2).wait_recv()
    c_core(2, 1).start()
    for d in (1, 2, 3):
        t_z(d).wait_recv()
    t_h.start()
    c_core(1, 1).wait_recv()
    attend_chunk(3)
    c_core(3, 1).wait_recv()
    attend_chunk(7)
    c_core(2, 0).wait_recv()
    attend_chunk(4)
    c_core(2, 1).wait_recv()
    attend_chunk(5)
    loop(heads, finish)
    t_h.wait_recv()
    for p in range(4):
        c_a(p).wait_send()
        c_b(p).wait_send()
        c_ay(p).wait_send()
    c_by.wait_send()
    for r in range(1, 8):
        c_core(r // 2, r % 2).wait_send()
    for d in (1, 2, 3):
        t_x(d).wait_send()
        t_z(d).wait_send()
    t_y.wait_send()
    t_c.wait_send()
    t_h.wait_send()


def project_kernel(heads, w_hbm, resid, gain, state, normed, w, wsem, *reduce_refs):
    pos = place()
    core, ylp, xs = exp_peers(pos)

    def load(n):
        return pltpu.make_async_copy(
            w_hbm.at[:, pl.ds(pl.multiple_of(n * W, W), W)], w.at[n], wsem.at[n]
        )

    loop(8, lambda n: load(n).start())
    greet([core, ylp] + xs)
    red = Reduce(reduce_refs, pos, True)

    def multiply(n):
        load(n).wait()
        t = jnp.dot(heads[...], w[n], preferred_element_type=F32)
        red.cs[n] = t[:128].astype(BF).reshape(4, 2, 16, W)
        red.c_core(n).start()
        red.own[n] = t[128:].reshape(4, 2, 16, W)

    def step(k):
        @when(k < 4)
        def _():
            multiply(2 * k)
            multiply(2 * k + 1)

        @when((k >= 1) & (k < 5))
        def _():
            red.first(k - 1)

        @when((k >= 2) & (k < 6))
        def _():
            red.second(k - 2)

        @when((k >= 3) & (k < 7))
        def _():
            red.carry(k - 3)

        @when(k >= 4)
        def _():
            red.third(k - 4)

    loop(8, step)
    square = jnp.zeros((16, 1), F32)
    for n in range(8):
        t = resid[:, n * W:(n + 1) * W].astype(F32) + red.acc[n]
        state[n] = t
        square = square + jnp.sum(t * t, axis=1, keepdims=True)
    scale = lax.rsqrt(square / (8 * W) + 1e-06)
    for n in range(8):
        normed[n] = (state[n] * scale * gain[:, n * W:(n + 1) * W]).astype(BF)
    loop(4, red.drain)


def experts_kernel(normed, table, state, wg_hbm, wd_hbm, out,
                   slots, weights, hits, wg, wd, wsem, xb, rows, abuf, fa, la, bbuf, bown, lb1, b2, fb, lb2, a2, la2, suma,
                   acta, actb, yrow, fin, ret, sems, *reduce_refs):
    pos = place()
    z, yh, x, yl, co = pos
    me = z * 2 + yh
    core, ylp, xs = exp_peers(pos)
    yo = (yl + 1) % 2
    yp = dev(z, (yh + 1) % 2, x, yl, co)
    zs = [dev((z + d) % 4, yh, x, yl, co) for d in (1, 2, 3)]
    red = ReduceX(reduce_refs, pos)
    (s_in, r_in, s_gy, r_gy, s_gx, r_gx, s_gc, r_gc,
     s_a1, r_a1, s_b1, r_b1, s_b2, r_b2, s_a2, r_a2, s_ay, r_ay, s_az, r_az, s_bz, r_bz, s_by, r_by,
     s_f, r_f) = sems
    na, nb = a2.shape[1], bown.shape[2]
    n1 = na - 48
    half = nb // 2
    above, below = zs[0], zs[2]

    loads = [
        pltpu.make_async_copy(wg_hbm.at[0], wg.at[0], wsem.at[0]),
        pltpu.make_async_copy(wg_hbm.at[1], wg.at[1], wsem.at[1]),
        pltpu.make_async_copy(wd_hbm, wd, wsem.at[2]),
    ]
    for cp in loads:
        cp.start()
    ctx = [dev((z + dz) % 4, (yh + dy) % 2, x, yl, co) for dz in range(4) for dy in range(2) if dz or dy]
    greet([core, ylp] + xs + ctx)

    def chunk(dz, dy):
        return ((z + 4 - dz) % 4) * 2 + (yh + dy) % 2

    def c_in(dz, dy):
        zz, yy = (z + dz) % 4, (yh + dy) % 2
        r = dz * 2 + dy
        return put(normed.at[zz * 2 + yy], xb.at[me, co, x, yl], s_in.at[r], r_in.at[r],
                   dev(zz, yy, x, yl, co))

    for dz in (1, 2, 3, 0):
        for dy in range(2):
            if dz or dy:
                c_in(dz, dy).start()
    xb[me, co, x, yl] = normed[me]

    def c_gy(dz, dy):
        c = chunk(dz, dy)
        return put(xb.at[c, co, x, yl], xb.at[c, co, x, yl], s_gy.at[dz, dy], r_gy.at[dz, dy], ylp)

    def c_gx(dz, dy, part):
        c = chunk(dz, dy)
        r = dz * 2 + dy
        src = x if part < 2 else (x + (3 if dy else 1)) % 4
        plus = part == 0 or (part == 2 and dy == 1)
        return put(xb.at[c, co, src], xb.at[c, co, src], s_gx.at[r, part], r_gx.at[r, part], xs[0 if plus else 2])

    def c_gc(dz, dy):
        c = chunk(dz, dy)
        return put(xb.at[c, co], xb.at[c, co], s_gc.at[dz, dy], r_gc.at[dz, dy], core)

    def gather1(dz):
        @when(dz > 0)
        def _():
            c_in(dz, 0).wait_recv()
        c_gy(dz, 0).start()
        c_in(dz, 1).wait_recv()
        c_gy(dz, 1).start()

    def gather2(dz):
        for dy in range(2):
            c_gy(dz, dy).wait_recv()
            c_gx(dz, dy, 0).start()
            c_gx(dz, dy, 1).start()

    def gather3(dz):
        for dy in range(2):
            c_gx(dz, dy, 0).wait_recv()
            c_gx(dz, dy, 1).wait_recv()
            c_gx(dz, dy, 2).start()

    def gather4(dz):
        for dy in range(2):
            c_gx(dz, dy, 2).wait_recv()
            c_gc(dz, dy).start()

    def c_far(g, dy):
        return put(abuf.at[g, 2, dy], fa.at[g, dy], s_a1.at[g, 0, dy], r_a1.at[g, 0, dy], above if dy else below)

    def c_below(g, dy):
        return put(abuf.at[g, 1, dy], la.at[g, 0, dy], s_a1.at[g, 1, dy], r_a1.at[g, 1, dy], below)

    def c_above(g, dy):
        return put(abuf.at[g, 3, dy], la.at[g, 1, dy], s_a1.at[g, 2, dy], r_a1.at[g, 2, dy], above)

    def c_b1(g, dz):
        return put(bbuf.at[g, dz], lb1.at[g, dz], s_b1.at[g, dz], r_b1.at[g, dz], yp)

    def part(h):
        return pl.ds(h * half, half)

    def c_bfar(g, h):
        return put(b2.at[g, 2, part(h)], fb.at[g, part(h)], s_b2.at[g, 0, h], r_b2.at[g, 0, h],
                   above if h else below)

    def c_bbelow(g, h):
        return put(b2.at[g, 1, part(h)], lb2.at[g, 0, part(h)], s_b2.at[g, 1, h], r_b2.at[g, 1, h], below)

    def c_babove(g, h):
        return put(b2.at[g, 3, part(h)], lb2.at[g, 1, part(h)], s_b2.at[g, 2, h], r_b2.at[g, 2, h], above)

    def c_a2(g):
        return put(a2.at[g], la2.at[g], s_a2.at[g], r_a2.at[g], yp)

    def c_ay(g):
        return put(acta.at[g, z, yh], acta.at[g, z, yh], s_ay.at[g], r_ay.at[g], yp)

    def c_az(g, p):
        if p < 2:
            src = acta.at[g, z]
        elif p == 2:
            src = acta.at[g, (z + 1) % 4, 0]
        else:
            src = acta.at[g, (z + 3) % 4, 1]
        return put(src, src, s_az.at[g, p], r_az.at[g, p], above if p in (0, 3) else below)

    def c_bz(g, p):
        if p < 2:
            src = actb.at[g, z, yh]
        elif p == 2:
            src = actb.at[g, (z + 1) % 4, yh, part(0)]
        else:
            src = actb.at[g, (z + 3) % 4, yh, part(1)]
        return put(src, src, s_bz.at[g, p], r_bz.at[g, p], above if p in (0, 3) else below)

    def c_by(g, dz):
        zz = (z + 4 - dz) % 4
        return put(actb.at[g, zz, yh], actb.at[g, zz, yh], s_by.at[g, dz], r_by.at[g, dz], yp)

    def find(k):
        for i in range(2):
            mine = table[k, :8, :] == (lax.axis_index("exp") * 2 + i).astype(F32)
            hits[k, i:i + 1, :] = jnp.max(jnp.where(mine, 1.0, 0.0), axis=0, keepdims=True)
            weights[k, i:i + 1, :] = jnp.sum(jnp.where(mine, table[k, 8:, :], 0.0), axis=0, keepdims=True)

    loop(8, find)
    one, two = (lax.broadcasted_iota(jnp.int32, (256, 256), a) for a in (0, 1))
    before = jnp.where((one < two) & (one // 16 == two // 16), 1.0, 0.0).astype(BF)
    block = (lax.broadcasted_iota(jnp.int32, (2, 256), 1) // 16 * 6).astype(F32)

    def rank(k):
        r = jnp.dot(hits[k].astype(BF), before, preferred_element_type=F32)
        slots[k] = jnp.where(hits[k] > 0.5, block + r, -1.0)

    loop(8, rank)
    row_id = lax.broadcasted_iota(jnp.int32, (48, 128), 0).astype(F32)

    def chosen(c, i, g):
        tokens = slice(g * 128, g * 128 + 128)
        return row_id == slots[c, i:i + 1, tokens] - 48.0 * g, weights[c, i:i + 1, tokens]

    def gate_up(dz):
        for dy in range(2):
            c_gc(dz, dy).wait_recv()
            c = chunk(dz, dy)
            for g in range(2):
                tokens = xb[c, g].reshape(128, W)
                for i in range(2):
                    pick = chosen(c, i, g)[0].astype(BF)
                    rows[i, g, dy * 48:(dy + 1) * 48] = jnp.dot(
                        pick, tokens, preferred_element_type=F32).astype(BF)

        def cols(t):
            sl = pl.ds(pl.multiple_of(t * 512, 512), 512)
            r = jnp.dot(rows[0].reshape(192, W), wg[0, :, sl], preferred_element_type=F32)
            abuf[:, dz, :, :48, sl] = r.astype(BF).reshape(2, 2, 48, 512)
            r = jnp.dot(rows[1].reshape(192, W), wg[1, :, sl], preferred_element_type=F32)
            r = r.astype(BF).reshape(2, 2, 48, 512)
            abuf[:, dz, :, 48:, sl] = r[:, :, :n1]
            bown[:, dz, :, sl] = r[:, 0, n1:]
            bbuf[:, dz, :, sl] = r[:, 1, n1:]

        loop(4, cols)

        @when(dz == 2)
        def _():
            c_far(0, 0).start()
            c_far(0, 1).start()

        @when(dz == 1)
        def _():
            c_below(0, 1).start()

        @when(dz == 3)
        def _():
            c_above(0, 0).start()

        c_b1(0, dz).start()

    def carry_a(g):
        for dy, dz, c in ((0, 1, c_below), (1, 3, c_above)):
            c_far(g, dy).wait_recv()

            def cols(t):
                sl = pl.ds(pl.multiple_of(t * 512, 512), 512)
                abuf[g, dz, dy, :, sl] = (abuf[g, dz, dy, :, sl].astype(F32) + fa[g, dy, :, sl].astype(F32)).astype(BF)

            loop(4, cols)
            c(g, dy).start()

    def forward_b(g):
        def one(dz):
            c_b1(g, dz).wait_recv()
            b2[g, dz] = (bown[g, dz].astype(F32) + lb1[g, dz].astype(F32)).astype(BF)

        loop(4, one)
        c_bfar(g, 0).start()
        c_bfar(g, 1).start()
        c_bbelow(g, 1).start()
        c_babove(g, 0).start()

    def carry_b(g):
        for h, dz, c in ((0, 1, c_bbelow), (1, 3, c_babove)):
            c_bfar(g, h).wait_recv()
            b2[g, dz, part(h)] = (b2[g, dz, part(h)].astype(F32) + fb[g, part(h)].astype(F32)).astype(BF)
            c(g, h).start()

    def sum_a(g):
        for dy in range(2):
            c_below(g, dy).wait_recv()
            c_above(g, dy).wait_recv()

        def cols(t):
            sl = pl.ds(pl.multiple_of(t * 512, 512), 512)

            def total(dy):
                r = abuf[g, 0, dy, :, sl].astype(F32)
                return r + la[g, 0, dy, :, sl].astype(F32) + la[g, 1, dy, :, sl].astype(F32)

            a2[g, :, sl] = total(1).astype(BF)
            suma[g, :, sl] = total(0)

        loop(4, cols)
        c_a2(g).start()

    def activate(gate, up):
        return (gate / (1.0 + jnp.exp(-gate)) * up).astype(BF)

    def halves(t):
        return tuple(pl.ds(pl.multiple_of(t * 256 + o, 256), 256) for o in (0, wd.shape[1]))

    def act_a(g):
        c_a2(g).wait_recv()

        def cols(t):
            def total(sl):
                return suma[g, :, sl] + la2[g, :, sl].astype(F32)

            lo, hi = halves(t)
            acta[g, z, yh, :, lo] = activate(total(lo), total(hi))

        loop(4, cols)
        c_ay(g).start()

    def act_b(g):
        for h in range(2):
            c_bbelow(g, h).wait_recv()
            c_babove(g, h).wait_recv()

        def cols(t):
            def total(sl):
                r = b2[g, 0, :, sl].astype(F32)
                return r + lb2[g, 0, :, sl].astype(F32) + lb2[g, 1, :, sl].astype(F32)

            lo, hi = halves(t)
            actb[g, z, yh, :, lo] = activate(total(lo), total(hi))

        loop(4, cols)
        c_bz(g, 0).start()
        c_bz(g, 1).start()
        c_by(g, 0).start()

    def spread_a(g):
        c_ay(g).wait_recv()
        c_az(g, 0).start()
        c_az(g, 1).start()

    def pass_on(g):
        for p in range(2):
            c_bz(g, p).wait_recv()
            c_bz(g, 3 - p).start()
        c_by(g, 1).start()
        c_by(g, 3).start()
        for p in range(2):
            c_az(g, p).wait_recv()
            c_az(g, 3 - p).start()

    def pass_far(g):
        c_bz(g, 2).wait_recv()
        c_bz(g, 3).wait_recv()
        c_by(g, 2).start()

    def order(k):
        return 2 - k + 3 * (k // 2) - 2 * (k // 3)

    def step(k):
        @when(k < 4)
        def _():
            gather1(order(k))

        @when((k >= 1) & (k < 5))
        def _():
            gather2(order(k - 1))

        @when((k >= 2) & (k < 6))
        def _():
            gather3(order(k - 2))

        @when(k == 4)
        def _():
            loads[0].wait()
            loads[1].wait()

        @when(k >= 4)
        def _():
            gate_up(order(k - 4))

        @when((k >= 3) & (k < 7))
        def _():
            gather4(order(k - 3))

    loop(8, step)
    def nearest(k):
        return k + k // 2 - 2 * (k // 3)

    def down(g, k):
        dz = nearest(k)
        zz = (z + 4 - dz) % 4

        if k == 3:
            c_az(g, 2).wait_recv()
            c_az(g, 3).wait_recv()
        c_by(g, dz).wait_recv()
        yrow[0] = jnp.dot(acta[g, zz, :, :48].reshape(96, -1), wd[0], preferred_element_type=F32).astype(BF)
        one = jnp.concatenate([acta[g, zz, :, 48:], actb[g, zz]], axis=1).reshape(96, -1)
        yrow[1] = jnp.dot(one, wd[1], preferred_element_type=F32).astype(BF)
        for dy in range(2):
            yy = (yh + dy) % 2
            c = zz * 2 + yy
            n = k * 2 + dy
            pick = jnp.concatenate([jnp.where(*chosen(c, i, g), 0.0) for i in range(2)], axis=0).astype(BF)
            sl = pl.ds(pl.multiple_of(yy * 48, 16), 48)
            t = lax.dot_general(
                pick, jnp.concatenate([yrow[0, sl], yrow[1, sl]], axis=0), (((0,), (0,)), ((), ())),
                preferred_element_type=F32).reshape(4, 2, 16, W)

            @when(co == g)
            def _():
                red.own[n] = t

            @when(co != g)
            def _():
                red.cs[n] = t.astype(BF)
                red.c_core(n).start()

    def c_f(k, dy):
        zz, yy = (z + 4 - nearest(k)) % 4, (yh + dy) % 2
        r = k * 2 + dy
        return put(fin.at[r], ret.at[me], s_f.at[r], r_f.at[r], dev(zz, yy, x, yl, co))

    def send_back(k):
        red.third(k)
        for dy in range(2):
            n = k * 2 + dy
            fin[n] = red.acc[n].astype(BF)
            if n:
                c_f(k, dy).start()

    def back(g, *stages):
        @when(co == g)
        def _():
            for stage, k in stages:
                stage(k)

    first, second, carry = red.first, red.second, red.carry
    carry_a(0)
    c_far(1, 0).start()
    c_far(1, 1).start()
    c_below(1, 1).start()
    c_above(1, 0).start()
    for dz in (2, 1, 3, 0):
        c_b1(1, dz).start()
    forward_b(0)
    sum_a(0)
    carry_b(0)
    act_a(0)
    carry_a(1)
    act_b(0)
    spread_a(0)
    forward_b(1)
    sum_a(1)
    carry_b(1)
    loads[2].wait()
    pass_on(0)
    down(0, 0)
    act_a(1)
    back(0, (first, 0))
    act_b(1)
    down(0, 1)
    spread_a(1)
    back(0, (second, 0), (first, 1))
    down(0, 2)
    back(0, (carry, 0), (second, 1), (first, 2))
    pass_far(0)
    down(0, 3)
    back(0, (send_back, 0), (carry, 1), (second, 2), (first, 3))
    pass_on(1)
    down(1, 0)
    back(0, (send_back, 1), (carry, 2), (second, 3))
    back(1, (first, 0))
    down(1, 1)
    back(0, (send_back, 2), (carry, 3))
    back(1, (second, 0), (first, 1))
    down(1, 2)
    back(0, (send_back, 3))
    back(1, (carry, 0), (second, 1), (first, 2))
    pass_far(1)
    down(1, 3)
    back(1, (send_back, 0), (carry, 1), (second, 2), (first, 3))
    back(1, (send_back, 1), (carry, 2), (second, 3))
    back(1, (send_back, 2), (carry, 3))
    back(1, (send_back, 3))
    ret[me] = fin[0]
    for r in range(1, 8):
        c_f(r // 2, r % 2).wait_recv()
    for n in range(8):
        out[:, n * W:(n + 1) * W] = (state[n] + ret[n].astype(F32)).astype(BF)

    loop(4, red.drain)
    for r in range(1, 8):
        c_f(r // 2, r % 2).wait_send()
        c_in(r // 2, r % 2).wait_send()
    for dz in range(4):
        for dy in range(2):
            for p in range(3):
                c_gx(dz, dy, p).wait_send()
            c_gy(dz, dy).wait_send()
            c_gc(dz, dy).wait_send()
        for g in range(2):
            c_b1(g, dz).wait_send()
            c_by(g, dz).wait_send()
    for g in range(2):
        for h in range(2):
            c_far(g, h).wait_send()
            c_below(g, h).wait_send()
            c_above(g, h).wait_send()
            c_bfar(g, h).wait_send()
            c_bbelow(g, h).wait_send()
            c_babove(g, h).wait_send()
        for p in range(4):
            c_az(g, p).wait_send()
            c_bz(g, p).wait_send()
        c_a2(g).wait_send()
        c_ay(g).wait_send()


VM = pl.BlockSpec(memory_space=pltpu.VMEM)
ANY = pl.BlockSpec(memory_space=pl.ANY)


def project(heads, w_out, resid, gain):
    return pl.pallas_call(
        project_kernel,
        name="project",
        out_shape=(jax.ShapeDtypeStruct((8, 16, W), F32), jax.ShapeDtypeStruct((8, 16, W), BF)),
        in_specs=[VM, ANY, VM, VM],
        out_specs=(VM, VM),
        scratch_shapes=[pltpu.VMEM((8, 768, W), BF), DMA((8,))] + REDUCE_SCRATCH,
        compiler_params=pltpu.CompilerParams(
            collective_id=1, has_side_effects=True, vmem_limit_bytes=50 << 20),
    )(heads, w_out, resid, gain)


def experts(normed, table, state, w_gate_up, w_down):
    hid2 = w_gate_up.shape[2]
    hid = hid2 // 2
    na, nb = 64, 32
    sems = [
        DMA((8,)), DMA((8,)),
        DMA((4, 2)), DMA((4, 2)), DMA((8, 3)), DMA((8, 3)),
        DMA((4, 2)), DMA((4, 2)),
        DMA((2, 3, 2)), DMA((2, 3, 2)), DMA((2, 4)), DMA((2, 4)), DMA((2, 3, 2)), DMA((2, 3, 2)),
        DMA((2,)), DMA((2,)), DMA((2,)), DMA((2,)), DMA((2, 4)), DMA((2, 4)), DMA((2, 4)), DMA((2, 4)),
        DMA((2, 4)), DMA((2, 4)),
        DMA((8,)), DMA((8,)),
    ]
    return pl.pallas_call(
        experts_kernel,
        name="experts",
        out_shape=jax.ShapeDtypeStruct((16, 8 * W), BF),
        in_specs=[VM, VM, VM, ANY, ANY],
        out_specs=VM,
        scratch_shapes=[
            pltpu.VMEM((8, 2, 256), F32),
            pltpu.VMEM((8, 2, 256), F32),
            pltpu.VMEM((8, 2, 256), F32),
            pltpu.VMEM((2, W, hid2), BF),
            pltpu.VMEM((2, hid, W), BF),
            DMA((3,)),
            pltpu.VMEM((8, 2, 4, 2, 16, W), BF),
            pltpu.VMEM((2, 2, 96, W), BF),
            pltpu.VMEM((2, 4, 2, na, hid2), BF),
            pltpu.VMEM((2, 2, na, hid2), BF),
            pltpu.VMEM((2, 2, 2, na, hid2), BF),
            pltpu.VMEM((2, 4, nb, hid2), BF),
            pltpu.VMEM((2, 4, nb, hid2), BF),
            pltpu.VMEM((2, 4, nb, hid2), BF),
            pltpu.VMEM((2, 4, nb, hid2), BF),
            pltpu.VMEM((2, nb, hid2), BF),
            pltpu.VMEM((2, 2, nb, hid2), BF),
            pltpu.VMEM((2, na, hid2), BF),
            pltpu.VMEM((2, na, hid2), BF),
            pltpu.VMEM((2, na, hid2), F32),
            pltpu.VMEM((2, 4, 2, na, hid), BF),
            pltpu.VMEM((2, 4, 2, nb, hid), BF),
            pltpu.VMEM((2, 96, W), BF),
            pltpu.VMEM((8, 16, W), BF),
            pltpu.VMEM((8, 16, W), BF),
            tuple(sems),
        ] + REDUCE_X_SCRATCH,
        compiler_params=pltpu.CompilerParams(
            collective_id=2, has_side_effects=True, vmem_limit_bytes=62 << 20),
    )(normed, table, state, w_gate_up, w_down)


def attend(block_order, queries, latent, w_uv, ids, weights):
    heads_dev, feat_width, query_count = queries.shape
    lat_width, value_width = w_uv.shape[1:]
    score_scale = (value_width + feat_width - lat_width) ** (-0.5)
    return pl.pallas_call(
        functools.partial(attend_kernel, score_scale * 1.4426950408889634),
        name="attend",
        out_shape=(
            jax.ShapeDtypeStruct((query_count, heads_dev * value_width), BF),
            jax.ShapeDtypeStruct((4, 2, 16, 256), F32),
        ),
        in_specs=[pl.BlockSpec(memory_space=pltpu.SMEM)] + [VM] * 5,
        out_specs=(VM, VM),
        scratch_shapes=[
            pltpu.VMEM((4, 2, 2, 128, (feat_width + 127) // 128 * 128), BF),
            pltpu.VMEM((2, 4, 2, 16, 128), BF),
            pltpu.VMEM((heads_dev, query_count, feat_width), BF),
            pltpu.VMEM((heads_dev, query_count, 128), F32),
            pltpu.VMEM((8, heads_dev, query_count, 256), F32),
            pltpu.VMEM((heads_dev, query_count, 128), F32),
            pltpu.VMEM((heads_dev, query_count, 128), F32),
            pltpu.VMEM((heads_dev, query_count, lat_width), F32),
            DMA((4,)), DMA((4,)), DMA((4,)), DMA((4,)), DMA((4,)), DMA((4,)), DMA, DMA,
            DMA((4, 2)), DMA((4, 2)),
            DMA((3,)), DMA((3,)), DMA, DMA, DMA, DMA, DMA((3,)), DMA((3,)), DMA, DMA,
        ],
        compiler_params=pltpu.CompilerParams(
            collective_id=3, has_side_effects=True, vmem_limit_bytes=40 << 20),
    )(block_order, queries, latent, w_uv, ids, weights)


def body(queries, latent, block_order, w_uv, w_out, resid, norm_gain, expert_ids, route_weights, w_gate_up, w_down):
    head_out, table = attend(
        block_order, queries.transpose(1, 2, 0), latent.T, w_uv, expert_ids.T, route_weights.T)
    table = table.reshape(8, 16, 256)
    state, normed = project(head_out, w_out, resid, norm_gain.reshape(1, -1))
    return experts(normed, table, state, w_gate_up, w_down)


def solution(mesh):
    return jax.shard_map(
        body,
        mesh=mesh,
        in_specs=(
            P("ctx", "exp", None),
            P("ctx", None),
            P(),
            P("exp", None, None),
            P("exp", None),
            P(("ctx", "exp"), None),
            P(),
            P(("ctx", "exp"), None),
            P(("ctx", "exp"), None),
            P("exp", "ctx", None),
            P("exp", None, "ctx"),
        ),
        out_specs=P(("ctx", "exp"), None),
        check_vma=False,
    )
```

time: 238 us -> 201 us (0.84)
  Pallas kernels: 224 us -> 189 us
    pallas_call x1, Pallas kernels: 54.1 us -> 32.6 us  [attend(): pl.pallas_call(functools.partial(attend_kernel, score_scale * 1.442695040...]
    pallas_call x1, Pallas kernels: 143 us -> 133 us  [experts(): pl.pallas_call(experts_kernel, name='experts', out_shape=jax.ShapeDtypeSt...]
    unnamed x21 -> x23, local copies, waits for them, and re-layouts: 7.41 us -> 11 us
    pallas_call x1, Pallas kernels: 27.3 us -> 24 us  [project(): pl.pallas_call(project_kernel, name='project', out_shape=(jax.ShapeDtypeS...]
where the time goes in v3:
time: 201 us; the launch traced here: 200 us
  Pallas kernels  189 us (94%)
  local copies, waits for them, and re-layouts  11 us (5%)
    pallas_call x1, Pallas kernels, experts(): pl.pallas_call(experts_kernel, name='experts', out_shape=jax.ShapeDtypeSt...  133 us
    pallas_call x1, Pallas kernels, attend(): pl.pallas_call(functools.partial(attend_kernel, score_scale * 1.442695040...  32.6 us
    pallas_call x1, Pallas kernels, project(): pl.pallas_call(project_kernel, name='project', out_shape=(jax.ShapeDtypeS...  24 us
    unnamed x23, local copies, waits for them, and re-layouts  11 us

profile of v3, /device:TPU:1, one launch (start us, length us, event | category | flops | bytes accessed | tf_op | source)
XLA Modules:
  0.0 200.4 jit_solution(9249238536196842206)
XLA Ops:
  0.0 0.0 copy-start
  0.0 1.5 copy-done
  1.5 0.0 copy-start.1
  1.5 1.1 copy-done.1
  2.6 0.0 copy-start.3
  2.6 1.0 copy-done.3
  3.6 0.0 copy-start.8
  3.6 0.7 copy-done.8
  4.3 0.0 copy-start.9
  4.3 0.7 copy-done.9
  4.9 0.0 copy-start.10
  5.0 0.7 copy-done.10
  5.6 32.6 %attend.1 = (bf16[256,768]{1,0:T(8,128)(2,1)S(1)}, f32[4,2,16,256]{3,2,1,0:T(8,128)S(1)}) custom-call(s32[16]{0:T(128)S(1)} %copy-done.10, bf16[6,576,256]{2,1,0:T(8,128)(2,1)S(1)} %bitcast.6, bf16[576,256]{1,0:T(8,128)(2,1)S(1)} %bitcast.7, bf16[6,512,128]{2,1,0:T(8,128)(2,1)S(1)} %copy-done.1, s32[8,16]{1,0:T(8,128)S(1)} %bitcast.10, f32[8,16]{1,0:T(8,128)S(1)} %bitcast.11), custom_call_target="tpu_custom_call" | custom-call | tf_op jit(solution)/shard_map/attend/pallas_call | solution.py:1067
  38.2 0.0 copy-start.6
  38.2 0.6 copy-done.6
  38.9 0.0 copy-start.4
  38.9 0.9 copy-done.4
  39.8 0.7 copy-done.7
  40.5 24.0 %project.1 = (f32[8,16,896]{2,1,0:T(8,128)S(1)}, bf16[8,16,896]{2,1,0:T(8,128)(2,1)S(1)}) custom-call(bf16[256,768]{1,0:T(8,128)(2,1)S(1)} %get-tuple-element.9.heads, bf16[768,7168]{1,0:T(8,128)(2,1)} %w_hbm.1, bf16[16,7168]{1,0:T(8,128)(2,1)S(1)} %copy-done.4, f32[1,7168]{1,0:T(1,128)S(1)} %bitcast.9), custom_call_target="tpu_custom_call" | custom-call | tf_op jit(solution)/shard_map/project/pallas_call | solution.py:999
  64.5 0.0 copy-start.2
  64.6 0.8 copy-done.2
  65.3 0.7 copy-done.5
  66.0 132.8 %experts.1 = bf16[16,7168]{1,0:T(8,128)(2,1)} custom-call(bf16[8,16,896]{2,1,0:T(8,128)(2,1)} %copy-done.5, f32[8,16,256]{2,1,0:T(8,128)} %bitcast.8, f32[8,16,896]{2,1,0:T(8,128)} %copy-done.2, bf16[2,896,2048]{2,1,0:T(8,128)(2,1)} %wg_hbm.1, bf16[2,1024,896]{2,1,0:T(8,128)(2,1)} %wd_hbm.1), custom_call_target="tpu_custom_call" | custom-call | tf_op jit(solution)/shard_map/experts/pallas_call | solution.py:1024
  198.8 1.6 copy.13
  (2 shorter events, 0.0 us)
Async XLA Ops:
  0.0 1.5 copy-start
  1.5 1.1 copy-start.1
  2.6 1.0 copy-start.3
  3.6 0.7 copy-start.8
  4.3 0.7 copy-start.9
  4.9 0.7 copy-start.10
  38.2 0.7 copy-start.6
  38.9 0.9 copy-start.4
  39.8 0.7 copy-start.7
  64.5 0.8 copy-start.2
  65.3 0.7 copy-start.5

commit v4 on v3

--- a/solution.py
+++ b/solution.py
@@ -276,7 +276,14 @@
     return pl.when(cond)
 
 
-def attend_kernel(scale, block_order, queries, latent, w_uv, ids, weights, out, table,
+def fetch(pairs, sems):
+    copies = [pltpu.make_async_copy(src, dst, sems.at[i]) for i, (src, dst) in enumerate(pairs)]
+    for cp in copies:
+        cp.start()
+    return copies
+
+
+def attend_part(scale, loads, block_order, queries, latent, w_uv, ids, weights, out, table,
                   kb, near, qs, top, scores, mid, part, some,
                   s_a, r_a, s_ay, r_ay, s_b, r_b, s_by, r_by, s_c, r_c,
                   s_tx, r_tx, s_ty, r_ty, s_tc, r_tc, s_tz, r_tz, s_th, r_th):
@@ -290,6 +297,7 @@
     heads = queries.shape[0]
     lat_width = w_uv.shape[1]
     greet([core, ylp, yp] + xs + zs)
+    got_latent, got_ids, got_weights, got_queries, got_w = loads
 
     def c_a(p):
         plane, first, count = ((0, 0, 64), (0, 0, 64), (1, 0, 32), (3, 32, 32))[p]
@@ -316,6 +324,7 @@
         src = kb.at[(z + 4 - dz) % 4, (yh + dy) % 2, co]
         return put(src, src, s_c.at[dz, dy], r_c.at[dz, dy], core)
 
+    got_latent.wait()
     kb[z, yh, :, :, feat:] = jnp.zeros((2, 128, kb.shape[4] - feat), BF)
     kb[z, yh, :, :, :feat] = latent[...].T.reshape(2, 128, feat)
     c_a(0).start()
@@ -323,6 +332,8 @@
     c_by.start()
     c_ay(0).start()
 
+    got_ids.wait()
+    got_weights.wait()
     near[co, x, yl] = jnp.zeros((16, 128), BF)
     near[co, x, yl, :, :16] = jnp.concatenate([ids[...].astype(F32), weights[...]], axis=0).astype(BF)
 
@@ -352,6 +363,7 @@
     def turn(h):
         qs[h] = queries[h].T
 
+    got_queries.wait()
     loop(heads, turn)
     top[...] = jnp.full(top.shape, -jnp.inf, F32)
 
@@ -456,6 +468,7 @@
     attend_chunk(4)
     c_core(2, 1).wait_recv()
     attend_chunk(5)
+    got_w.wait()
     loop(heads, finish)
     t_h.wait_recv()
     for p in range(4):
@@ -473,17 +486,8 @@
     t_h.wait_send()
 
 
-def project_kernel(heads, w_hbm, resid, gain, state, normed, w, wsem, *reduce_refs):
+def project_part(heads, load, last, resid, gain, state, normed, w, *reduce_refs):
     pos = place()
-    core, ylp, xs = exp_peers(pos)
-
-    def load(n):
-        return pltpu.make_async_copy(
-            w_hbm.at[:, pl.ds(pl.multiple_of(n * W, W), W)], w.at[n], wsem.at[n]
-        )
-
-    loop(8, lambda n: load(n).start())
-    greet([core, ylp] + xs)
     red = Reduce(reduce_refs, pos, True)
 
     def multiply(n):
@@ -516,6 +520,8 @@
             red.third(k - 4)
 
     loop(8, step)
+    for cp in last:
+        cp.wait()
     square = jnp.zeros((16, 1), F32)
     for n in range(8):
         t = resid[:, n * W:(n + 1) * W].astype(F32) + red.acc[n]
@@ -527,8 +533,32 @@
     loop(4, red.drain)
 
 
-def experts_kernel(normed, table, state, wg_hbm, wd_hbm, out,
-                   slots, weights, hits, wg, wd, wsem, xb, rows, abuf, fa, la, bbuf, bown, lb1, b2, fb, lb2, a2, la2, suma,
+ATTEND_SEMS = [
+    DMA((4,)), DMA((4,)), DMA((4,)), DMA((4,)), DMA((4,)), DMA((4,)), DMA, DMA,
+    DMA((4, 2)), DMA((4, 2)),
+    DMA((3,)), DMA((3,)), DMA, DMA, DMA, DMA, DMA((3,)), DMA((3,)), DMA, DMA,
+]
+
+
+def front_kernel(scale, block_order, queries_hbm, latent_hbm, w_uv_hbm, ids_hbm, weights_hbm, w_hbm, resid_hbm,
+                 gain_hbm, state, normed, table, queries, latent, w_uv, ids, weights, resid, gain, heads, w,
+                 lsem, wsem, *refs):
+    loads = fetch([(latent_hbm, latent), (ids_hbm, ids), (weights_hbm, weights), (queries_hbm, queries),
+                   (w_uv_hbm, w_uv), (resid_hbm, resid), (gain_hbm, gain)], lsem)
+
+    def load(n):
+        return pltpu.make_async_copy(
+            w_hbm.at[:, pl.ds(pl.multiple_of(n * W, W), W)], w.at[n], wsem.at[n]
+        )
+
+    loop(8, lambda n: load(n).start())
+    count = 8 + len(ATTEND_SEMS)
+    attend_part(scale, loads[:5], block_order, queries, latent, w_uv, ids, weights, heads, table, *refs[:count])
+    project_part(heads, load, loads[5:], resid, gain, state, normed, w, *refs[count:])
+
+
+def experts_kernel(normed_hbm, table_hbm, state_hbm, wg_hbm, wd_hbm, out,
+                   normed, table, state, lsem, slots, weights, hits, wg, wd, wsem, xb, rows, abuf, fa, la, bbuf, bown, lb1, b2, fb, lb2, a2, la2, suma,
                    acta, actb, yrow, fin, ret, sems, *reduce_refs):
     pos = place()
     z, yh, x, yl, co = pos
@@ -546,6 +576,8 @@
     half = nb // 2
     above, below = zs[0], zs[2]
 
+    got_normed, got_table, got_state = fetch(
+        [(normed_hbm, normed), (table_hbm, table), (state_hbm, state)], lsem)
     loads = [
         pltpu.make_async_copy(wg_hbm.at[0], wg.at[0], wsem.at[0]),
         pltpu.make_async_copy(wg_hbm.at[1], wg.at[1], wsem.at[1]),
@@ -553,8 +585,10 @@
     ]
     for cp in loads:
         cp.start()
-    ctx = [dev((z + dz) % 4, (yh + dy) % 2, x, yl, co) for dz in range(4) for dy in range(2) if dz or dy]
+    ctx = [dev((z + dz) % 4, (yh + dy) % 2, x, yy, co)
+           for dz in range(4) for dy in range(2) for yy in (yl, yo) if dz or dy]
     greet([core, ylp] + xs + ctx)
+    got_normed.wait()
 
     def chunk(dz, dy):
         return ((z + 4 - dz) % 4) * 2 + (yh + dy) % 2
@@ -565,15 +599,18 @@
         return put(normed.at[zz * 2 + yy], xb.at[me, co, x, yl], s_in.at[r], r_in.at[r],
                    dev(zz, yy, x, yl, co))
 
-    for dz in (1, 2, 3, 0):
+    xb[me, co, x, yl] = normed[me]
+
+    def c_gy(dz, dy):
+        zz, yy = (z + dz) % 4, (yh + dy) % 2
+        return put(normed.at[zz * 2 + yy], xb.at[me, co, x, yl], s_gy.at[dz, dy], r_gy.at[dz, dy],
+                   dev(zz, yy, x, yo, co))
+
+    for dz in (2, 1, 3, 0):
         for dy in range(2):
             if dz or dy:
                 c_in(dz, dy).start()
-    xb[me, co, x, yl] = normed[me]
-
-    def c_gy(dz, dy):
-        c = chunk(dz, dy)
-        return put(xb.at[c, co, x, yl], xb.at[c, co, x, yl], s_gy.at[dz, dy], r_gy.at[dz, dy], ylp)
+            c_gy(dz, dy).start()
 
     def c_gx(dz, dy, part):
         c = chunk(dz, dy)
@@ -590,9 +627,7 @@
         @when(dz > 0)
         def _():
             c_in(dz, 0).wait_recv()
-        c_gy(dz, 0).start()
         c_in(dz, 1).wait_recv()
-        c_gy(dz, 1).start()
 
     def gather2(dz):
         for dy in range(2):
@@ -670,6 +705,7 @@
             hits[k, i:i + 1, :] = jnp.max(jnp.where(mine, 1.0, 0.0), axis=0, keepdims=True)
             weights[k, i:i + 1, :] = jnp.sum(jnp.where(mine, table[k, 8:, :], 0.0), axis=0, keepdims=True)
 
+    got_table.wait()
     loop(8, find)
     one, two = (lax.broadcasted_iota(jnp.int32, (256, 256), a) for a in (0, 1))
     before = jnp.where((one < two) & (one // 16 == two // 16), 1.0, 0.0).astype(BF)
@@ -940,23 +976,24 @@
     back(0, (carry, 0), (second, 1), (first, 2))
     pass_far(0)
     down(0, 3)
-    back(0, (send_back, 0), (carry, 1), (second, 2), (first, 3))
     pass_on(1)
     down(1, 0)
-    back(0, (send_back, 1), (carry, 2), (second, 3))
+    back(0, (send_back, 0), (carry, 1), (second, 2), (first, 3))
     back(1, (first, 0))
     down(1, 1)
-    back(0, (send_back, 2), (carry, 3))
     back(1, (second, 0), (first, 1))
     down(1, 2)
-    back(0, (send_back, 3))
     back(1, (carry, 0), (second, 1), (first, 2))
+    back(0, (send_back, 1), (carry, 2), (second, 3))
     pass_far(1)
     down(1, 3)
-    back(1, (send_back, 0), (carry, 1), (second, 2), (first, 3))
-    back(1, (send_back, 1), (carry, 2), (second, 3))
-    back(1, (send_back, 2), (carry, 3))
+    back(1, (first, 3), (send_back, 0), (carry, 1), (second, 2))
+    back(0, (send_back, 2), (carry, 3))
+    back(1, (second, 3), (send_back, 1), (carry, 2))
+    back(1, (carry, 3), (send_back, 2))
     back(1, (send_back, 3))
+    back(0, (send_back, 3))
+    got_state.wait()
     ret[me] = fin[0]
     for r in range(1, 8):
         c_f(r // 2, r % 2).wait_recv()
@@ -995,19 +1032,6 @@
 ANY = pl.BlockSpec(memory_space=pl.ANY)
 
 
-def project(heads, w_out, resid, gain):
-    return pl.pallas_call(
-        project_kernel,
-        name="project",
-        out_shape=(jax.ShapeDtypeStruct((8, 16, W), F32), jax.ShapeDtypeStruct((8, 16, W), BF)),
-        in_specs=[VM, ANY, VM, VM],
-        out_specs=(VM, VM),
-        scratch_shapes=[pltpu.VMEM((8, 768, W), BF), DMA((8,))] + REDUCE_SCRATCH,
-        compiler_params=pltpu.CompilerParams(
-            collective_id=1, has_side_effects=True, vmem_limit_bytes=50 << 20),
-    )(heads, w_out, resid, gain)
-
-
 def experts(normed, table, state, w_gate_up, w_down):
     hid2 = w_gate_up.shape[2]
     hid = hid2 // 2
@@ -1025,9 +1049,13 @@
         experts_kernel,
         name="experts",
         out_shape=jax.ShapeDtypeStruct((16, 8 * W), BF),
-        in_specs=[VM, VM, VM, ANY, ANY],
+        in_specs=[ANY] * 5,
         out_specs=VM,
         scratch_shapes=[
+            pltpu.VMEM(normed.shape, BF),
+            pltpu.VMEM(table.shape, F32),
+            pltpu.VMEM(state.shape, F32),
+            DMA((3,)),
             pltpu.VMEM((8, 2, 256), F32),
             pltpu.VMEM((8, 2, 256), F32),
             pltpu.VMEM((8, 2, 256), F32),
@@ -1060,20 +1088,32 @@
     )(normed, table, state, w_gate_up, w_down)
 
 
-def attend(block_order, queries, latent, w_uv, ids, weights):
+def front(block_order, queries, latent, w_uv, ids, weights, w_out, resid, gain):
     heads_dev, feat_width, query_count = queries.shape
     lat_width, value_width = w_uv.shape[1:]
     score_scale = (value_width + feat_width - lat_width) ** (-0.5)
     return pl.pallas_call(
-        functools.partial(attend_kernel, score_scale * 1.4426950408889634),
-        name="attend",
+        functools.partial(front_kernel, score_scale * 1.4426950408889634),
+        name="front",
         out_shape=(
-            jax.ShapeDtypeStruct((query_count, heads_dev * value_width), BF),
+            jax.ShapeDtypeStruct((8, 16, W), F32),
+            jax.ShapeDtypeStruct((8, 16, W), BF),
             jax.ShapeDtypeStruct((4, 2, 16, 256), F32),
         ),
-        in_specs=[pl.BlockSpec(memory_space=pltpu.SMEM)] + [VM] * 5,
-        out_specs=(VM, VM),
+        in_specs=[pl.BlockSpec(memory_space=pltpu.SMEM)] + [ANY] * 8,
+        out_specs=(VM, VM, VM),
         scratch_shapes=[
+            pltpu.VMEM(queries.shape, BF),
+            pltpu.VMEM(latent.shape, BF),
+            pltpu.VMEM(w_uv.shape, BF),
+            pltpu.VMEM(ids.shape, jnp.int32),
+            pltpu.VMEM(weights.shape, F32),
+            pltpu.VMEM(resid.shape, BF),
+            pltpu.VMEM(gain.shape, F32),
+            pltpu.VMEM((query_count, heads_dev * value_width), BF),
+            pltpu.VMEM((8, 768, W), BF),
+            DMA((7,)),
+            DMA((8,)),
             pltpu.VMEM((4, 2, 2, 128, (feat_width + 127) // 128 * 128), BF),
             pltpu.VMEM((2, 4, 2, 16, 128), BF),
             pltpu.VMEM((heads_dev, query_count, feat_width), BF),
@@ -1082,21 +1122,17 @@
             pltpu.VMEM((heads_dev, query_count, 128), F32),
             pltpu.VMEM((heads_dev, query_count, 128), F32),
             pltpu.VMEM((heads_dev, query_count, lat_width), F32),
-            DMA((4,)), DMA((4,)), DMA((4,)), DMA((4,)), DMA((4,)), DMA((4,)), DMA, DMA,
-            DMA((4, 2)), DMA((4, 2)),
-            DMA((3,)), DMA((3,)), DMA, DMA, DMA, DMA, DMA((3,)), DMA((3,)), DMA, DMA,
-        ],
+        ] + ATTEND_SEMS + REDUCE_SCRATCH,
         compiler_params=pltpu.CompilerParams(
-            collective_id=3, has_side_effects=True, vmem_limit_bytes=40 << 20),
-    )(block_order, queries, latent, w_uv, ids, weights)
+            collective_id=3, has_side_effects=True, vmem_limit_bytes=62 << 20),
+    )(block_order, queries, latent, w_uv, ids, weights, w_out, resid, gain)
 
 
 def body(queries, latent, block_order, w_uv, w_out, resid, norm_gain, expert_ids, route_weights, w_gate_up, w_down):
-    head_out, table = attend(
-        block_order, queries.transpose(1, 2, 0), latent.T, w_uv, expert_ids.T, route_weights.T)
-    table = table.reshape(8, 16, 256)
-    state, normed = project(head_out, w_out, resid, norm_gain.reshape(1, -1))
-    return experts(normed, table, state, w_gate_up, w_down)
+    state, normed, table = front(
+        block_order, queries.transpose(1, 2, 0), latent.T, w_uv, expert_ids.T, route_weights.T,
+        w_out, resid, norm_gain.reshape(1, -1))
+    return experts(normed, table.reshape(8, 16, 256), state, w_gate_up, w_down)
 
 
 def solution(mesh):

time: 201 us -> 186 us (0.925)
  local copies, waits for them, and re-layouts: 11 us -> 1.64 us
  Pallas kernels: 189 us -> 184 us
    unnamed x23 -> x1, local copies, waits for them, and re-layouts: 11 us -> 1.64 us
    pallas_call x1, Pallas kernels: 133 us -> 128 us  [experts(): pl.pallas_call(experts_kernel, name='experts', out_shape=jax.ShapeDtypeSt...]
    pallas_call x2 -> x1, Pallas kernels: 56.6 us -> 56.6 us  [front(): pl.pallas_call(functools.partial(front_kernel, score_scale * 1.4426950408...]
where the time goes in v4:
time: 186 us
  Pallas kernels  184 us (99%)
    pallas_call x1, Pallas kernels, experts(): pl.pallas_call(experts_kernel, name='experts', out_shape=jax.ShapeDtypeSt...  128 us
    pallas_call x1, Pallas kernels, front(): pl.pallas_call(functools.partial(front_kernel, score_scale * 1.4426950408...  56.6 us

profile of v4, /device:TPU:1, one launch (start us, length us, event | category | flops | bytes accessed | tf_op | source)
XLA Modules:
  0.0 185.9 jit_solution(6098166838249510262)
XLA Ops:
  0.0 56.6 %front.1 = (f32[8,16,896]{2,1,0:T(8,128)}, bf16[8,16,896]{2,1,0:T(8,128)(2,1)}, f32[4,2,16,256]{3,2,1,0:T(8,128)}) custom-call(s32[16]{0:T(128)} %block_order.1, bf16[6,576,256]{2,1,0:T(8,128)(2,1)} %bitcast.6, bf16[576,256]{1,0:T(8,128)(2,1)} %bitcast.7, bf16[6,512,128]{2,1,0:T(8,128)(2,1)} %w_uv_hbm.1, s32[8,16]{1,0:T(8,128)} %bitcast.10, ...), custom_call_target="tpu_custom_call" | custom-call | tf_op jit(solution)/shard_map/front/pallas_call | solution.py:1095
  56.6 127.7 %experts.1 = bf16[16,7168]{1,0:T(8,128)(2,1)} custom-call(bf16[8,16,896]{2,1,0:T(8,128)(2,1)} %get-tuple-element.8.normed_hbm, f32[8,16,256]{2,1,0:T(8,128)} %bitcast.8, f32[8,16,896]{2,1,0:T(8,128)} %get-tuple-element.10.state_hbm, bf16[2,896,2048]{2,1,0:T(8,128)(2,1)} %wg_hbm.1, bf16[2,1024,896]{2,1,0:T(8,128)(2,1)} %wd_hbm.1), custom_call_target="tpu_custom_call" | custom-call | tf_op jit(solution)/shard_map/experts/pallas_call | solution.py:1048
  184.3 1.6 copy.13

commit v5 on v4

--- a/solution.py
+++ b/solution.py
@@ -55,6 +55,7 @@
     pltpu.VMEM((8, 4, 2, 16, W), BF),
     pltpu.VMEM((8, 4, 2, 16, W), BF),
     pltpu.VMEM((4, 3, 2, 16, W), BF),
+    pltpu.VMEM((4, 2, 16, W), BF),
     pltpu.VMEM((8, 4, 16, W), BF),
     pltpu.VMEM((4, 16, W), BF),
     pltpu.VMEM((8, 3, 16, W), BF),
@@ -76,7 +77,7 @@
 
 class Reduce:
     def __init__(self, refs, pos, crossed):
-        (self.own, self.cs, self.cl, self.s1, self.x1, self.y1, self.y2s, self.x2s, self.y2,
+        (self.own, self.cs, self.cl, self.s1, self.x1, self.xc, self.y1, self.y2s, self.x2s, self.y2,
          self.x2, self.acc, *self.sems) = refs
         self.pos = pos
         self.crossed = crossed
@@ -85,10 +86,16 @@
     def c_core(self, n):
         return put(self.cs.at[n], self.cl.at[n], self.sems[0].at[n], self.sems[1].at[n], self.core)
 
-    def c_x1(self, i, d):
-        xx = (self.pos[2] + d) % 4
-        return put(self.s1.at[2 * i, xx], self.x1.at[i, d - 1], self.sems[2].at[i, d - 1],
-                   self.sems[3].at[i, d - 1], self.xs[d - 1])
+    def c_x1(self, i, part):
+        z, yh, x, yl, co = self.pos
+        way = 1 + 2 * (i % 2)
+        if part == 2:
+            src = self.xc.at[i]
+        else:
+            src = self.s1.at[2 * i, (x + (2 if part == 0 else 4 - way)) % 4]
+        to = (x + (4 - way if part == 1 else way)) % 4
+        return put(src, self.x1.at[i, part], self.sems[2].at[i, part], self.sems[3].at[i, part],
+                   dev(z, yh, to, yl, co))
 
     def c_y1(self, n):
         return put(self.s1.at[n, :, (self.pos[3] + 1) % 2], self.y1.at[n], self.sems[4].at[n],
@@ -111,8 +118,8 @@
             self.c_core(n).wait_recv()
             self.s1[n] = (self.own[n] + self.cl[n].astype(F32)).astype(BF)
             if self.crossed and j == 0:
-                for d in (1, 2, 3):
-                    self.c_x1(i, d).start()
+                self.c_x1(i, 0).start()
+                self.c_x1(i, 1).start()
             else:
                 self.c_y1(n).start()
 
@@ -121,18 +128,10 @@
         for j in range(2):
             n = 2 * i + j
             if self.crossed and j == 0:
-                for d in (1, 2, 3):
-                    self.c_x1(i, d).wait_recv()
-
-                def over_x(which):
-                    t = self.s1[n, x, which].astype(F32)
-                    for d in (0, 1, 2):
-                        t = t + self.x1[i, d, which].astype(F32)
-                    return t
-
-                self.y2s[i] = over_x((yl + 1) % 2).astype(BF)
-                self.c_y2(i).start()
-                self.acc[n] = over_x(yl)
+                self.c_x1(i, 0).wait_recv()
+                near = (x + 1 + 2 * (i % 2)) % 4
+                self.xc[i] = (self.s1[n, near].astype(F32) + self.x1[i, 0].astype(F32)).astype(BF)
+                self.c_x1(i, 2).start()
             else:
                 self.c_y1(n).wait_recv()
                 for part, d in ((0, 2), (1, 1 if j else 3)):
@@ -143,7 +142,18 @@
     def carry(self, i):
         for j in range(2):
             n = 2 * i + j
-            if not (self.crossed and j == 0):
+            if self.crossed and j == 0:
+                self.c_x1(i, 1).wait_recv()
+                self.c_x1(i, 2).wait_recv()
+
+                def over_x(which):
+                    t = self.s1[n, self.pos[2], which].astype(F32)
+                    return t + self.x1[i, 1, which].astype(F32) + self.x1[i, 2, which].astype(F32)
+
+                self.y2s[i] = over_x((self.pos[3] + 1) % 2).astype(BF)
+                self.c_y2(i).start()
+                self.acc[n] = over_x(self.pos[3])
+            else:
                 self.c_x2(n, 0, j == 1).wait_recv()
                 xx = (self.pos[2] + (3 if j else 1)) % 4
                 self.x2s[n, 2] = (self.over_y(n, xx) + self.x2[n, 0].astype(F32)).astype(BF)
@@ -172,7 +182,7 @@
                 self.c_y1(n).wait_send()
             for d in (1, 2, 3):
                 if self.crossed and j == 0:
-                    self.c_x1(i, d).wait_send()
+                    self.c_x1(i, d - 1).wait_send()
                 else:
                     self.c_x2(n, d - 1, j == 1).wait_send()
 
@@ -411,7 +421,6 @@
             row = (g % 2 + co + 1) % 2 * 128 + g // 2 * 16
             out[pl.ds(pl.multiple_of(row, 16), 16), cols] = r[g * 16:g * 16 + 16]
 
-    attend_chunk(0)
     c_by.wait_recv()
     c_b(0).start()
     c_b(1).start()
@@ -423,6 +432,7 @@
     c_a(1).wait_recv()
     c_a(2).start()
     c_ay(3).start()
+    attend_chunk(0)
     for d in (1, 2, 3):
         t_x(d).wait_recv()
     t_y.start()
@@ -624,8 +634,7 @@
         return put(xb.at[c, co], xb.at[c, co], s_gc.at[dz, dy], r_gc.at[dz, dy], core)
 
     def gather1(dz):
-        @when(dz > 0)
-        def _():
+        if dz:
             c_in(dz, 0).wait_recv()
         c_in(dz, 1).wait_recv()
 
@@ -866,33 +875,23 @@
     def order(k):
         return 2 - k + 3 * (k // 2) - 2 * (k // 3)
 
+    for dz in (2, 1, 3, 0):
+        gather1(dz)
+        gather2(dz)
+    gather3(order(0))
+    loads[0].wait()
+    loads[1].wait()
+
     def step(k):
-        @when(k < 4)
+        @when(k < 3)
         def _():
-            gather1(order(k))
-
-        @when((k >= 1) & (k < 5))
-        def _():
-            gather2(order(k - 1))
-
-        @when((k >= 2) & (k < 6))
-        def _():
-            gather3(order(k - 2))
-
-        @when(k == 4)
-        def _():
-            loads[0].wait()
-            loads[1].wait()
-
-        @when(k >= 4)
-        def _():
-            gate_up(order(k - 4))
-
-        @when((k >= 3) & (k < 7))
-        def _():
-            gather4(order(k - 3))
-
-    loop(8, step)
+            gather3(order(k + 1))
+
+        gather4(order(k))
+        gate_up(order(k))
+
+    loop(4, step)
+
     def nearest(k):
         return k + k // 2 - 2 * (k // 3)
 

time: 186 us -> 185 us (level)
    pallas_call x1, Pallas kernels: 56.6 us -> 54.6 us  [front(): pl.pallas_call(functools.partial(front_kernel, score_scale * 1.4426950408...]
where the time goes in v5:
time: 185 us
  Pallas kernels  183 us (99%)
    pallas_call x1, Pallas kernels, experts(): pl.pallas_call(experts_kernel, name='experts', out_shape=jax.ShapeDtypeSt...  129 us
    pallas_call x1, Pallas kernels, front(): pl.pallas_call(functools.partial(front_kernel, score_scale * 1.4426950408...  54.6 us

profile of v5, /device:TPU:1, one launch (start us, length us, event | category | flops | bytes accessed | tf_op | source)
XLA Modules:
  0.0 185.1 jit_solution(8043802244447023780)
XLA Ops:
  0.0 54.6 %front.1 = (f32[8,16,896]{2,1,0:T(8,128)}, bf16[8,16,896]{2,1,0:T(8,128)(2,1)}, f32[4,2,16,256]{3,2,1,0:T(8,128)}) custom-call(s32[16]{0:T(128)} %block_order.1, bf16[6,576,256]{2,1,0:T(8,128)(2,1)} %bitcast.6, bf16[576,256]{1,0:T(8,128)(2,1)} %bitcast.7, bf16[6,512,128]{2,1,0:T(8,128)(2,1)} %w_uv_hbm.1, s32[8,16]{1,0:T(8,128)} %bitcast.10, ...), custom_call_target="tpu_custom_call" | custom-call | tf_op jit(solution)/shard_map/front/pallas_call | solution.py:1094
  54.6 128.9 %experts.1 = bf16[16,7168]{1,0:T(8,128)(2,1)} custom-call(bf16[8,16,896]{2,1,0:T(8,128)(2,1)} %get-tuple-element.8.normed_hbm, f32[8,16,256]{2,1,0:T(8,128)} %bitcast.8, f32[8,16,896]{2,1,0:T(8,128)} %get-tuple-element.10.state_hbm, bf16[2,896,2048]{2,1,0:T(8,128)(2,1)} %wg_hbm.1, bf16[2,1024,896]{2,1,0:T(8,128)(2,1)} %wd_hbm.1), custom_call_target="tpu_custom_call" | custom-call | tf_op jit(solution)/shard_map/experts/pallas_call | solution.py:1047
  183.5 1.6 copy.13

commit v6 on v5

--- a/solution.py
+++ b/solution.py
@@ -768,6 +768,7 @@
             c_above(0, 0).start()
 
         c_b1(0, dz).start()
+        c_b1(1, dz).start()
 
     def carry_a(g):
         for dy, dz, c in ((0, 1, c_below), (1, 3, c_above)):
@@ -950,8 +951,6 @@
     c_far(1, 1).start()
     c_below(1, 1).start()
     c_above(1, 0).start()
-    for dz in (2, 1, 3, 0):
-        c_b1(1, dz).start()
     forward_b(0)
     sum_a(0)
     carry_b(0)

time: 185 us -> 186 us (level)
  no operation moved by 1% of the time
where the time goes in v6:
time: 186 us; the launch traced here: 185 us
  Pallas kernels  184 us (99%)
    pallas_call x1, Pallas kernels, experts(): pl.pallas_call(experts_kernel, name='experts', out_shape=jax.ShapeDtypeSt...  129 us
    pallas_call x1, Pallas kernels, front(): pl.pallas_call(functools.partial(front_kernel, score_scale * 1.4426950408...  54.6 us

profile of v6, /device:TPU:1, one launch (start us, length us, event | category | flops | bytes accessed | tf_op | source)
XLA Modules:
  0.0 185.5 jit_solution(4074751273670625644)
XLA Ops:
  0.0 54.6 %front.1 = (f32[8,16,896]{2,1,0:T(8,128)}, bf16[8,16,896]{2,1,0:T(8,128)(2,1)}, f32[4,2,16,256]{3,2,1,0:T(8,128)}) custom-call(s32[16]{0:T(128)} %block_order.1, bf16[6,576,256]{2,1,0:T(8,128)(2,1)} %bitcast.6, bf16[576,256]{1,0:T(8,128)(2,1)} %bitcast.7, bf16[6,512,128]{2,1,0:T(8,128)(2,1)} %w_uv_hbm.1, s32[8,16]{1,0:T(8,128)} %bitcast.10, ...), custom_call_target="tpu_custom_call" | custom-call | tf_op jit(solution)/shard_map/front/pallas_call | solution.py:1093
  54.6 129.3 %experts.1 = bf16[16,7168]{1,0:T(8,128)(2,1)} custom-call(bf16[8,16,896]{2,1,0:T(8,128)(2,1)} %get-tuple-element.8.normed_hbm, f32[8,16,256]{2,1,0:T(8,128)} %bitcast.8, f32[8,16,896]{2,1,0:T(8,128)} %get-tuple-element.10.state_hbm, bf16[2,896,2048]{2,1,0:T(8,128)(2,1)} %wg_hbm.1, bf16[2,1024,896]{2,1,0:T(8,128)(2,1)} %wd_hbm.1), custom_call_target="tpu_custom_call" | custom-call | tf_op jit(solution)/shard_map/experts/pallas_call | solution.py:1046
  183.8 1.6 copy.13
